TPU v7x, 32 devices: a whole 2x2x4 slice. The times are simulated.
32 devices in a mesh: gx: 4 (over y, core), gy: 8 (over z, x).
Axes of the slice: x: 2, y: 2, z: 4, core: 2. Of those that a mesh axis runs over, the one named last changes fastest.
Arguments:
- tracer_adjoint: float32 [2, 50, 320, 512], P(None, None, 'gy', 'gx'), may hold values from -6 to 6
- surface_adjoint: float32 [320, 512], P('gy', 'gx'), may hold values from -6 to 6
- flow_east: float32 [50, 320, 512], P(None, 'gy', 'gx'), may hold values from -0.4 to 0.4, as said below
- flow_north: float32 [50, 320, 512], P(None, 'gy', 'gx'), may hold values from -0.4 to 0.4, as said below
- vertical_mix: float32 [49, 320, 512], P(None, 'gy', 'gx'), may hold values from 0.1 to 10
- land_mask: int32 [50, 320, 512], P(None, 'gy', 'gx'), may hold values from 0 to 1, as said below
- conduct_east: float32 [320, 512], P('gy', 'gx'), may hold values from 0 to 4, as said below
- conduct_north: float32 [320, 512], P('gy', 'gx'), may hold values from 0 to 4, as said below
- surface_diagonal: float32 [320, 512], P('gy', 'gx'), may hold values from 0.02 to 0.2
- pressure_load: float32 [2, 50], replicated, may hold values from -0.5 to 0.5
- surface_forcing: float32 [2, 50], replicated, may hold values from -0.1 to 0.1
- control_map: int32 [1664], replicated, may hold values from 0 to 319
- control_weight: float32 [1664], replicated, may hold values from 0.5 to 1.5
Outputs:
- tracer_grad: float32 [2, 50, 320, 512], P(None, None, 'gy', 'gx')
- surface_grad: float32 [320, 512], P('gy', 'gx')
- control_grad: float32 [2, 50, 320], P(None, None, ('gx', 'gy'))
Inputs may be any that keep to these rules, and one draw needn't show every extreme that they name: `land_mask`: 1 marks an ocean cell and 0 land; where a cell is ocean, the cell above it is ocean too. `flow_east`: zero on every face that touches land or lies on the grid's eastern edge. `flow_north`: zero on every face that touches land or lies on the grid's northern edge. `conduct_east`: zero on faces that touch land at the surface or lie on the eastern edge, positive elsewhere. `conduct_north`: zero on faces that touch land at the surface or lie on the northern edge, positive elsewhere.
All inputs are finite; a program needn't handle non-finite values.
Results may differ from a plain program's by a relative error of at most 0.0003.
Values sent between devices are 32-bit elements; how exact they have to be, the bound alone decides.
A program may use at most 128 MiB of HBM per device.

v0:
```python
import jax
import jax.numpy as jnp
from jax import lax
from jax.sharding import PartitionSpec as P

ITERS = 3
CTRL_DEV = 10


def passed_along(value, axis, steps):
    count = lax.axis_size(axis)
    leading, last = (max(0, -steps), min(count, count - steps))
    return lax.ppermute(value, axis, [(source, source + steps) for source in range(leading, last)])


def extended(shard, sides, width):
    for axis, dim in sides:
        peers, length = (lax.axis_size(axis), shard.shape[dim])
        up = [(i, (i + 1) % peers) for i in range(peers - 1)]
        down = [(j, i) for i, j in up]
        last = lax.slice_in_dim(shard, length - width, length, axis=dim)
        leading = lax.slice_in_dim(shard, 0, width, axis=dim)
        before = lax.ppermute(last, axis, up)
        after = lax.ppermute(leading, axis, down)
        shard = jnp.concatenate([before, shard, after], axis=dim)
    return shard


def column_solve(right_side, kappa_vert):
    levels = right_side.shape[-3]
    ratios = []
    reduced = []
    for level in range(levels):
        diag_term = 1.0
        if level > 0:
            diag_term = diag_term + kappa_vert[level - 1]
        if level < levels - 1:
            diag_term = diag_term + kappa_vert[level]
        if level == 0:
            pivot_val = diag_term
            carried = right_side[..., 0, :, :]
        else:
            pivot_val = diag_term - kappa_vert[level - 1] * ratios[level - 1]
            carried = right_side[..., level, :, :] + kappa_vert[level - 1] * reduced[level - 1]
        reduced.append(carried / pivot_val)
        if level < levels - 1:
            ratios.append(kappa_vert[level] / pivot_val)
    solution = [reduced[levels - 1]]
    for level in range(levels - 2, -1, -1):
        solution.insert(0, reduced[level] + ratios[level] * solution[0])
    return jnp.stack(solution, axis=-3)


def squares(remain):
    return lax.psum(jnp.sum(remain * remain), ("gx", "gy"))


def per_device(
    tracer_adjoint,
    surface_adjoint,
    flow_east,
    flow_north,
    vertical_mix,
    land_mask,
    conduct_east,
    conduct_north,
    surface_diagonal,
    pressure_load,
    surface_forcing,
    control_map,
    control_weight,
):
    wet_cells = land_mask.astype(jnp.float32)
    tiles_lon = lax.axis_size("gx")
    tiles_lat = lax.axis_size("gy")
    tile_col = lax.axis_index("gx")
    tile_row = lax.axis_index("gy")
    levels, rows_here, cols_here = flow_east.shape
    west_rim = passed_along(
        jnp.concatenate([flow_east[:, :, -1:], conduct_east[None, :, -1:]], axis=0), "gx", 1
    )
    flow_west = jnp.concatenate([west_rim[:levels], flow_east[:, :, :-1]], axis=2)
    conduct_west = jnp.concatenate([west_rim[levels], conduct_east[:, :-1]], axis=1)
    south_rim = passed_along(
        jnp.concatenate([flow_north[:, -1:, :], conduct_north[None, -1:, :]], axis=0), "gy", 1
    )
    flow_south = jnp.concatenate([south_rim[:levels], flow_north[:, :-1, :]], axis=1)
    conduct_south = jnp.concatenate([south_rim[levels], conduct_north[:-1, :]], axis=0)
    kappa_vert = vertical_mix * wet_cells[1:]
    loads = wet_cells[None] * pressure_load[:, :, None, None]
    forcing_sum = surface_adjoint + jnp.sum(
        surface_forcing[:, :, None, None] * wet_cells[None] * tracer_adjoint, axis=(0, 1)
    )
    iterate = jnp.zeros_like(forcing_sum)
    remain = forcing_sum
    search = remain
    norm_now = squares(remain)
    for iteration in range(ITERS):
        padded = extended(search, (("gx", 1), ("gy", 0)), 1)
        surface_east_side = padded[1:-1, 2:]
        surface_west_side = padded[1:-1, :-2]
        surface_north_side = padded[2:, 1:-1]
        surface_south_side = padded[:-2, 1:-1]
        image = (
            surface_diagonal * search
            + conduct_east * (search - surface_east_side)
            + conduct_west * (search - surface_west_side)
            + conduct_north * (search - surface_north_side)
            + conduct_south * (search - surface_south_side)
        )
        step_len = norm_now / lax.psum(jnp.sum(search * image), ("gx", "gy"))
        iterate = iterate + step_len * search
        remain = remain - step_len * image
        if iteration + 1 < ITERS:
            norm_next = squares(remain)
            search = remain + norm_next / norm_now * search
            norm_now = norm_next
    lifted = tracer_adjoint + loads * iterate[None, None]
    lambda_pad = extended(
        wet_cells[None] * column_solve(lifted, kappa_vert), (("gx", 3), ("gy", 2)), 1
    )
    center = lambda_pad[..., 1:-1, 1:-1]
    east_side = lambda_pad[..., 1:-1, 2:]
    west_side = lambda_pad[..., 1:-1, :-2]
    north_side = lambda_pad[..., 2:, 1:-1]
    south_side = lambda_pad[..., :-2, 1:-1]
    tracer_grad = (
        center
        + 0.5 * flow_east * (east_side - center)
        + 0.5 * flow_west * (center - west_side)
        + 0.5 * flow_north * (north_side - center)
        + 0.5 * flow_south * (center - south_side)
    )
    lon_cells = cols_here * tiles_lon
    lat_cells = rows_here * tiles_lat
    share_len = CTRL_DEV
    control_count = share_len * tiles_lon * tiles_lat
    edge_vals = jnp.concatenate(
        [
            tracer_grad[:, :, 0, :],
            tracer_grad[:, :, -1, :],
            tracer_grad[:, :, :, 0],
            tracer_grad[:, :, :, -1],
        ],
        axis=2,
    )
    begins = [
        tile_col * cols_here,
        lon_cells + tile_col * cols_here,
        2 * lon_cells + tile_row * rows_here,
        2 * lon_cells + lat_cells + tile_row * rows_here,
    ]
    amounts = [cols_here, cols_here, rows_here, rows_here]
    actives = [tile_row == 0, tile_row == tiles_lat - 1, tile_col == 0, tile_col == tiles_lon - 1]
    point_ids = jnp.concatenate(
        [
            lax.dynamic_slice_in_dim(control_map, begin, amount)
            for begin, amount in zip(begins, amounts)
        ]
    )
    point_wts = jnp.concatenate(
        [
            lax.dynamic_slice_in_dim(control_weight, begin, amount) * active.astype(jnp.float32)
            for begin, amount, active in zip(begins, amounts, actives)
        ]
    )
    weighted = (edge_vals * point_wts).reshape(2 * levels, -1)
    onehot = (point_ids[:, None] == jnp.arange(control_count, dtype=jnp.int32)[None, :]).astype(
        jnp.float32
    )
    contribution = jnp.dot(
        weighted, onehot, precision=lax.Precision.HIGHEST, preferred_element_type=jnp.float32
    ).reshape(2, levels, control_count)
    totals = lax.psum(contribution, ("gx", "gy"))
    owner_idx = tile_col * tiles_lat + tile_row
    control_grad = lax.dynamic_slice_in_dim(totals, owner_idx * share_len, share_len, 2)
    return (tracer_grad, iterate, control_grad)


def solution(mesh):
    in_specs = (
        P(None, None, "gy", "gx"),
        P("gy", "gx"),
        P(None, "gy", "gx"),
        P(None, "gy", "gx"),
        P(None, "gy", "gx"),
        P(None, "gy", "gx"),
        P("gy", "gx"),
        P("gy", "gx"),
        P("gy", "gx"),
        P(),
        P(),
        P(),
        P(),
    )
    out_specs = (P(None, None, "gy", "gx"), P("gy", "gx"), P(None, None, ("gx", "gy")))
    return jax.shard_map(
        per_device, mesh=mesh, in_specs=in_specs, out_specs=out_specs, check_vma=False
    )
```

profile of v0, /device:TPU:0, one launch (start us, length us, event | category | flops | bytes accessed | tf_op | source)
XLA Modules:
  0.0 540.0 jit_solution(16159869313040959848)
XLA Ops:
  8.6 4.1 multiply_reduce_fusion
  14.7 3.6 collective-permute-start.2
  19.9 4.5 collective-permute-start.1
  26.0 4.0 collective-permute-start.4
  58.2 4.5 collective-permute-start.5
  65.8 41.6 %all-reduce = (f32[]{:T(128)}, f32[]{:T(128)}) all-reduce(f32[]{:T(128)} %get-tuple-element.13, f32[]{:T(128)} %get-tuple-element.12), channel_id=1, replica_groups=mesh['gx'=4,'gy'=8] {'gx','gy'}, use_global_device_ids=true, to_apply=%region_2.0 | all-reduce | flops 2 | bytes 16 | tf_op jit(solution)/shard_map/psum | solution.py:55
  109.3 40.3 %psum.51 = f32[]{:T(128)} all-reduce(f32[]{:T(128)} %get-tuple-element.159), channel_id=1, replica_groups=mesh['gx'=4,'gy'=8] {'gx','gy'}, use_global_device_ids=true, to_apply=%region_6.0 | all-reduce | flops 1 | bytes 8 | tf_op jit(solution)/shard_map/psum | solution.py:55
  152.3 3.0 collective-permute-start.7
  157.6 4.8 collective-permute-start.9
  165.1 44.2 %psum.52 = f32[]{:T(128)} all-reduce(f32[]{:T(128)} %get-tuple-element.157), channel_id=1, replica_groups=mesh['gx'=4,'gy'=8] {'gx','gy'}, use_global_device_ids=true, to_apply=%region_8.0 | all-reduce | flops 1 | bytes 8 | tf_op jit(solution)/shard_map/psum | solution.py:111
  212.1 40.8 %psum.53 = f32[]{:T(128)} all-reduce(f32[]{:T(128)} %multiply_reduce_fusion.1), channel_id=1, replica_groups=mesh['gx'=4,'gy'=8] {'gx','gy'}, use_global_device_ids=true, to_apply=%region_10.0 | all-reduce | flops 1 | bytes 8 | tf_op jit(solution)/shard_map/psum | solution.py:55
  255.6 3.0 collective-permute-start.11
  261.4 5.4 collective-permute-start.13
  269.5 2.5 copy.200
  274.6 2.3 copy.203
  276.9 42.2 %psum.54 = f32[]{:T(128)} all-reduce(f32[]{:T(128)} %fusion.102), channel_id=1, replica_groups=mesh['gx'=4,'gy'=8] {'gx','gy'}, use_global_device_ids=true, to_apply=%region_12.0 | all-reduce | flops 1 | bytes 8 | tf_op jit(solution)/shard_map/psum | solution.py:111
  320.8 4.0 multiply_add_fusion
  325.3 5.7 %add_divide_fusion.3 = (f32[2,1,40,128]{3,0,2,1:T(2,128)S(1)}, f32[2,1,40,128]{3,0,2,1:T(2,128)S(1)}, f32[2,1,40,128]{3,0,2,1:T(2,128)S(1)}, f32[2,1,40,128]{3,0...) fusion(f32[2,50,40,128]{3,0,2,1:T(2,128)S(1)} %multiply_add_fus, ...), kind=kLoop, calls=%fused_computation.238 | loop fusion | flops 1177600 | bytes 4730880 | tf_op jit(solution)/shard_map/div | solution.py:45
  331.4 4.7 fusion.21
  336.4 5.1 constant_dynamic-update-slice_fusion.49
  344.9 4.2 fusion.199
  349.2 3.7 copy.201
  354.1 3.7 copy.205
  357.8 3.0 collective-permute-start.15
  364.4 3.0 copy.202
  367.4 3.1 copy.206
  373.3 4.8 collective-permute-start.17
  379.1 3.2 collective-permute-done.17
  382.3 13.0 %fusion.2 = f32[2,50,40,128]{3,0,1,2:T(2,128)S(1)} fusion(f32[2,50,40,128]{3,0,1,2:T(2,128)S(1)} %broadcast_multiply_fusion, f32[2,50,1,130]{3,0,1,2:T(2,128)S(1)} %collective-permute-done.17, f32[2,50,40,1]{3,0,1,2:T(2,128)S(1)} %copy-done.2, f32[2,50,40,1]{3,0,1,2:T(2,128)S(1)} %copy-done.3, f32[2,50,1,130]{3,0,1,2:T(2,128)S(1)} %collective-permute-done.16, ...), kind=kLoop, calls=%fused_computation.3 | loop fusion | flops 10240000 | bytes 8328000 | tf_op jit(solution)/shard_map/add | solution.py:128
  395.4 3.5 fusion.198
  400.3 3.8 copy.213
  407.0 124.7 %all-reduce.3.cloned.1.call-done = f32[2,50,320]{1,2,0:T(8,128)} async-done(((f32[2,50,320]{1,2,0:T(8,128)}), f32[2,50,320]{1,2,0:T(8,128)}) %all-reduce.3.cloned.1.call-update) | async-done | bytes 128016 | tf_op jit(solution)/shard_map/psum | solution.py:174
  (421 shorter events, 72.9 us)
Async XLA Ops:
  7.2 524.6 %all-reduce.3.cloned.1.call-start = ((), (), s32[]{:S(2)}) async-start(), calls=%async_computation | async-start | bytes 655360 | tf_op jit(solution)/shard_map/psum | solution.py:174
  12.7 12.7 %copy-start.13 = (f32[40,128]{1,0:T(8,128)S(1)}, f32[40,128]{1,0:T(8,128)}, u32[]{:S(2)}) copy-start(f32[40,128]{1,0:T(8,128)} %param.20) | copy-start | bytes 61444
  13.5 42.6 %collective-permute-start = (f32[40,1]{1,0:T(8,128)}, f32[40,1]{1,0:T(8,128)}, u32[]{:S(2)}, u32[]{:S(2)}) collective-permute-start(f32[40,1]{1,0:T(8,128)} %get-tuple-element.256), channel_id=1, source_target_pairs={{8,0},{16,8},{24,16},{9,1},{17,9},{25,17},{10,2},{18,10},{26,18},{... | collective-permute-start | bytes 488 | tf_op jit(solution)/shard_map/ppermute | solution.py:24
  14.7 41.4 %collective-permute-start.2 = (f32[40,1]{1,0:T(8,128)}, f32[40,1]{1,0:T(8,128)}, u32[]{:S(2)}, u32[]{:S(2)}) collective-permute-start(f32[40,1]{1,0:T(8,128)} %get-tuple-element.255), channel_id=1, source_target_pairs={{0,8},{8,16},{16,24},{1,9},{9,17},{17,25},{2,10},{10,18},{18,26},{... | collective-permute-start | bytes 488 | tf_op jit(solution)/shard_map/ppermute | solution.py:23
  19.9 42.8 %collective-permute-start.1 = (f32[51,40,1]{0,1,2:T(8,128)}, f32[51,40,1]{0,1,2:T(8,128)}, u32[]{:S(2)}, u32[]{:S(2)}) collective-permute-start(f32[51,40,1]{0,1,2:T(8,128)} %pad_maximum_fusion.36), channel_id=1, source_target_pairs={{0,8},{8,16},{16,24},{1,9},{9,17},{17,25},{2,10},{10,18},{18,26},{... | collective-permute-start | bytes 24488 | tf_op jit(solution)/shard_map/ppermute | solution.py:13
  26.0 37.5 %collective-permute-start.4 = (f32[51,1,128]{2,0,1:T(8,128)}, f32[51,1,128]{2,0,1:T(8,128)}, u32[]{:S(2)}, u32[]{:S(2)}) collective-permute-start(f32[51,1,128]{2,0,1:T(8,128)} %pad_maximum_fusion.11), channel_id=1, source_target_pairs={{0,1},{1,2},{2,3},{3,4},{4,5},{5,6},{6,7},{8,9},{9,10},{10,11},{11... | collective-permute-start | bytes 78344 | tf_op jit(solution)/shard_map/ppermute | solution.py:13
  33.1 14.0 %copy-start.81 = (f32[40,128]{1,0:T(8,128)}, f32[40,128]{1,0:T(8,128)S(1)}, u32[]{:S(2)}) copy-start(f32[40,128]{1,0:T(8,128)S(1)} %get-tuple-element.107) | copy-start | bytes 61444
  35.9 11.2 %copy-start.20 = (f32[1,40,128]{2,1,0:T(8,128)}, f32[1,40,128]{2,1,0:T(8,128)S(1)}, u32[]{:S(2)}) copy-start(f32[1,40,128]{2,1,0:T(8,128)S(1)} %get-tuple-element.51) | copy-start | bytes 61444
  35.9 11.2 %copy-start.46 = (f32[1,40,128]{2,1,0:T(8,128)}, f32[1,40,128]{2,1,0:T(8,128)S(1)}, u32[]{:S(2)}) copy-start(f32[1,40,128]{2,1,0:T(8,128)S(1)} %get-tuple-element.50) | copy-start | bytes 61444
  36.5 11.2 %copy-start.22 = (f32[1,40,128]{2,1,0:T(8,128)}, f32[1,40,128]{2,1,0:T(8,128)S(1)}, u32[]{:S(2)}) copy-start(f32[1,40,128]{2,1,0:T(8,128)S(1)} %get-tuple-element.54) | copy-start | bytes 61444
  37.2 11.1 %copy-start.50 = (f32[1,40,128]{2,1,0:T(8,128)}, f32[1,40,128]{2,1,0:T(8,128)S(1)}, u32[]{:S(2)}) copy-start(f32[1,40,128]{2,1,0:T(8,128)S(1)} %get-tuple-element.56) | copy-start | bytes 61444
  40.5 15.6 %copy-start.14 = (f32[1,40,128]{2,1,0:T(8,128)}, f32[1,40,128]{2,1,0:T(8,128)S(1)}, u32[]{:S(2)}) copy-start(f32[1,40,128]{2,1,0:T(8,128)S(1)} %get-tuple-element.72) | copy-start | bytes 61444
  41.3 24.5 %copy-start.16 = (f32[1,40,128]{2,1,0:T(8,128)}, f32[1,40,128]{2,1,0:T(8,128)S(1)}, u32[]{:S(2)}) copy-start(f32[1,40,128]{2,1,0:T(8,128)S(1)} %get-tuple-element.75) | copy-start | bytes 61444
  42.6 20.2 %copy-start.34 = (f32[1,40,128]{2,1,0:T(8,128)}, f32[1,40,128]{2,1,0:T(8,128)S(1)}, u32[]{:S(2)}) copy-start(f32[1,40,128]{2,1,0:T(8,128)S(1)} %get-tuple-element.81) | copy-start | bytes 61444
  43.2 119.9 %copy-start.36 = (f32[1,40,128]{2,1,0:T(8,128)}, f32[1,40,128]{2,1,0:T(8,128)S(1)}, u32[]{:S(2)}) copy-start(f32[1,40,128]{2,1,0:T(8,128)S(1)} %get-tuple-element.84) | copy-start | bytes 61444
  56.9 7.4 %collective-permute-start.3 = (f32[1,130]{1,0:T(1,128)S(1)}, f32[1,130]{1,0:T(1,128)S(1)}, u32[]{:S(2)}, u32[]{:S(2)}) collective-permute-start(f32[1,130]{1,0:T(1,128)S(1)} %get-tuple-element.249), channel_id=1, source_target_pairs={{1,0},{2,1},{3,2},{4,3},{5,4},{6,5},{7,6},{9,8},{10,9},{11,10},{12... | collective-permute-start | bytes 1568 | tf_op jit(solution)/shard_map/ppermute | solution.py:24
  58.2 6.1 %collective-permute-start.5 = (f32[1,130]{1,0:T(1,128)S(1)}, f32[1,130]{1,0:T(1,128)S(1)}, u32[]{:S(2)}, u32[]{:S(2)}) collective-permute-start(f32[1,130]{1,0:T(1,128)S(1)} %get-tuple-element.250), channel_id=1, source_target_pairs={{0,1},{1,2},{2,3},{3,4},{4,5},{5,6},{6,7},{8,9},{9,10},{10,11},{11... | collective-permute-start | bytes 1568 | tf_op jit(solution)/shard_map/ppermute | solution.py:23
  151.0 5.2 collective-permute-start.6
  152.3 3.9 collective-permute-start.7
  156.3 6.8 %collective-permute-start.8 = (f32[1,130]{1,0:T(1,128)S(1)}, f32[1,130]{1,0:T(1,128)S(1)}, u32[]{:S(2)}, u32[]{:S(2)}) collective-permute-start(f32[1,130]{1,0:T(1,128)S(1)} %get-tuple-element.247), channel_id=1, source_target_pairs={{1,0},{2,1},{3,2},{4,3},{5,4},{6,5},{7,6},{9,8},{10,9},{11,10},{12... | collective-permute-start | bytes 1568 | tf_op jit(solution)/shard_map/ppermute | solution.py:24
  157.6 6.1 %collective-permute-start.9 = (f32[1,130]{1,0:T(1,128)S(1)}, f32[1,130]{1,0:T(1,128)S(1)}, u32[]{:S(2)}, u32[]{:S(2)}) collective-permute-start(f32[1,130]{1,0:T(1,128)S(1)} %get-tuple-element.248), channel_id=1, source_target_pairs={{0,1},{1,2},{2,3},{3,4},{4,5},{5,6},{6,7},{8,9},{9,10},{10,11},{11... | collective-permute-start | bytes 1568 | tf_op jit(solution)/shard_map/ppermute | solution.py:23
  254.3 5.2 collective-permute-start.10
  255.6 3.9 collective-permute-start.11
  260.1 13.1 %collective-permute-start.12 = (f32[1,130]{1,0:T(1,128)}, f32[1,130]{1,0:T(1,128)}, u32[]{:S(2)}, u32[]{:S(2)}) collective-permute-start(f32[1,130]{1,0:T(1,128)} %get-tuple-element.245), channel_id=1, source_target_pairs={{1,0},{2,1},{3,2},{4,3},{5,4},{6,5},{7,6},{9,8},{10,9},{11,10},{12... | collective-permute-start | bytes 1568 | tf_op jit(solution)/shard_map/ppermute | solution.py:24
  261.4 11.8 %collective-permute-start.13 = (f32[1,130]{1,0:T(1,128)}, f32[1,130]{1,0:T(1,128)}, u32[]{:S(2)}, u32[]{:S(2)}) collective-permute-start(f32[1,130]{1,0:T(1,128)} %get-tuple-element.246), channel_id=1, source_target_pairs={{0,1},{1,2},{2,3},{3,4},{4,5},{5,6},{6,7},{8,9},{9,10},{10,11},{11... | collective-permute-start | bytes 1568 | tf_op jit(solution)/shard_map/ppermute | solution.py:23
  352.8 11.6 %collective-permute-start.14 = (f32[2,50,40,1]{1,2,3,0:T(8,128)S(1)}, f32[2,50,40,1]{1,2,3,0:T(8,128)S(1)}, u32[]{:S(2)}, u32[]{:S(2)}) collective-permute-start(f32[2,50,40,1]{1,2,3,0:T(8,128)S(1)} %copy.201), channel_id=1, source_target_pairs={{8,0},{16,8},{24,16},{9,1},{17,9},{25,17},{10,2},{18,10},{26,18},{... | collective-permute-start | bytes 48008 | tf_op jit(solution)/shard_map/ppermute | solution.py:24
  357.8 9.6 %collective-permute-start.15 = (f32[2,50,40,1]{1,2,3,0:T(8,128)S(1)}, f32[2,50,40,1]{1,2,3,0:T(8,128)S(1)}, u32[]{:S(2)}, u32[]{:S(2)}) collective-permute-start(f32[2,50,40,1]{1,2,3,0:T(8,128)S(1)} %copy.205), channel_id=1, source_target_pairs={{0,8},{8,16},{16,24},{1,9},{9,17},{17,25},{2,10},{10,18},{18,26},{... | collective-permute-start | bytes 48008 | tf_op jit(solution)/shard_map/ppermute | solution.py:23
  370.6 11.7 %copy-start.6 = (f32[50,40,128]{2,0,1:T(8,128)S(1)}, f32[50,40,128]{2,0,1:T(8,128)}, u32[]{:S(2)}) copy-start(f32[50,40,128]{2,0,1:T(8,128)} %copy.200) | copy-start | bytes 3072004
  370.6 11.7 %copy-start.7 = (f32[50,40,128]{2,0,1:T(8,128)S(1)}, f32[50,40,128]{2,0,1:T(8,128)}, u32[]{:S(2)}) copy-start(f32[50,40,128]{2,0,1:T(8,128)} %copy.207) | copy-start | bytes 3072004
  370.6 11.7 %copy-start.8 = (f32[50,40,128]{2,0,1:T(8,128)S(1)}, f32[50,40,128]{2,0,1:T(8,128)}, u32[]{:S(2)}) copy-start(f32[50,40,128]{2,0,1:T(8,128)} %copy.204) | copy-start | bytes 3072004
  372.0 7.1 %collective-permute-start.16 = (f32[2,50,1,130]{3,0,1,2:T(2,128)S(1)}, f32[2,50,1,130]{3,0,1,2:T(2,128)S(1)}, u32[]{:S(2)}, u32[]{:S(2)}) collective-permute-start(f32[2,50,1,130]{3,0,1,2:T(2,128)S(1)} %get-tuple-element.162), channel_id=1, source_target_pairs={{1,0},{2,1},{3,2},{4,3},{5,4},{6,5},{7,6},{9,8},{10,9},{11,10},{12... | collective-permute-start | bytes 156008 | tf_op jit(solution)/shard_map/ppermute | solution.py:24
  373.3 9.0 %collective-permute-start.17 = (f32[2,50,1,130]{3,0,1,2:T(2,128)S(1)}, f32[2,50,1,130]{3,0,1,2:T(2,128)S(1)}, u32[]{:S(2)}, u32[]{:S(2)}) collective-permute-start(f32[2,50,1,130]{3,0,1,2:T(2,128)S(1)} %get-tuple-element.163), channel_id=1, source_target_pairs={{0,1},{1,2},{2,3},{3,4},{4,5},{5,6},{6,7},{8,9},{9,10},{10,11},{11... | collective-permute-start | bytes 156008 | tf_op jit(solution)/shard_map/ppermute | solution.py:23
  (118 other events, 567.6 us)
Sparse Core Ops, SparseCore 0:
  405.7 126.0 all-reduce.2
where the time goes:
time: 543 us; the launch traced here: 540 us
  blocking collectives  209 us (38%)
  waiting for transfers between devices  129 us (24%)
  other arithmetic  78.5 us (14%)
  starting transfers between devices  51.1 us (9%)
  local copies, waits for them, and re-layouts  48.2 us (9%)
  between operations  22.9 us (4%)
    psum x1, waiting for transfers between devices, per_device(): totals = lax.psum(contribution, ('gx', 'gy'))  125 us
    psum x3, blocking collectives, squares(): return lax.psum(jnp.sum(remain * remain), ('gx', 'gy'))  123 us
    psum x2, blocking collectives, per_device(): step_len = norm_now / lax.psum(jnp.sum(search * image), ('gx', 'gy'))  86.5 us
    ppermute x8, starting transfers between devices, extended(): before = lax.ppermute(last, axis, up)  32.3 us
    mul x21, other arithmetic, column_solve(): solution.insert(0, reduced[level] + ratios[level] * solution[0])  15.3 us
    add x1, other arithmetic, per_device(): center + 0.5 * flow_east * (east_side - center)  13 us
    div x3, other arithmetic, column_solve(): reduced.append(carried / pivot_val)  11.8 us
  transfers between devices with their start and end apart: 19, of which 4 were waited for; matrix products, arithmetic and copies ran while one was open for 9% of the time, Pallas kernels for 0%

commit v1 on v0

v1 whole, which is shorter than its diff:
```python
import functools
import jax
import jax.numpy as jnp
from jax import lax
from jax.experimental import pallas as pl
from jax.experimental.pallas import tpu as pltpu
from jax.sharding import PartitionSpec as P

ITERS = 3
CTRL_DEV = 10
SLOT = 16
LANES = 128
MESH = pl.DeviceIdType.MESH
DIRS = ((1, 0), (-1, 0), (0, 1), (0, -1), (1, 1), (-1, 1), (1, -1), (-1, -1))
OPPOSITE = (1, 0, 3, 2, 7, 6, 5, 4)
F32 = jnp.float32
HIGHEST = lax.Precision.HIGHEST


def column_roll(value, shift):
    return pltpu.roll(value, shift, 1)


def surface_apply(e, ce, cn, dg):
    rows, cols = e.shape
    flux_e = ce * (e - pltpu.roll(e, cols - 1, 1))
    flux_n = cn * (e - pltpu.roll(e, rows - 1, 0))
    return dg * e + (flux_e - pltpu.roll(flux_e, 1, 1)) + (flux_n - pltpu.roll(flux_n, 1, 0))


def poly_add(p, q, factor):
    size = max(len(p), len(q))
    out = []
    for i in range(size):
        term = factor * q[i] if i < len(q) else None
        if i < len(p):
            term = p[i] if term is None else p[i] + term
        out.append(term)
    return out


def gradient_weights(mu):
    def inner(p, q, shift):
        total = None
        for i, pi in enumerate(p):
            for j, qj in enumerate(q):
                term = pi * qj * mu[i + j + shift]
                total = term if total is None else total + term
        return total

    one = jnp.ones_like(mu[0])
    zero = jnp.zeros_like(mu[0])
    floor = 2e-7 * mu[0]
    res, search, x = [one], [one], [zero]
    rr = mu[0]
    for it in range(ITERS):
        den = inner(search, search, 1)
        good = (den > 0) & (rr > floor)
        step = jnp.where(good, rr / jnp.where(good, den, one), zero)
        x = poly_add(x, search, step)
        if it + 1 < ITERS:
            res = poly_add(res, [zero] + search, -step)
            rr_new = jnp.maximum(inner(res, res, 0), zero)
            ratio = jnp.where(good, rr_new / jnp.where(good, rr, one), zero)
            search = poly_add(res, search, ratio)
            rr = rr_new
    return x


def step_kernel(
    tiles_lon, tiles_lat, levels,
    tracer, surface, flow_e, flow_n, mix, mask, cond_e, cond_n, diag, load, forcing, cmap, cwt,
    grad_out, surf_out, ctrl_out,
    red, ratio, quad, q_e, q_w, q_n, q_s, q_c,
    send_e, send_w, send_n, send_s, recv_e, recv_w, recv_n, recv_s,
    mom_send, mom_y, mom_x_send, mom_x,
    edge_s, edge_n, edge_w, edge_e,
    ctl_send, ctl_x, ctl_y_send, ctl_y,
    hs, hr, ls, lr, mys, myr, mxs, mxr, cxs, cxr, cys, cyr,
):
    col = lax.axis_index("gx")
    row = lax.axis_index("gy")
    cy, cx = surface.shape
    pack = edge_s.shape[0]
    has = []
    for dx, dy in DIRS:
        ok = None
        for d, pos, size in ((dx, col, tiles_lon), (dy, row, tiles_lat)):
            if d:
                here = (pos < size - 1) if d > 0 else (pos > 0)
                ok = here if ok is None else ok & here
        has.append(ok)

    barrier = pltpu.get_barrier_semaphore()
    for d in range(1, tiles_lon):
        pl.semaphore_signal(barrier, inc=1, device_id=(lax.rem(col + d, tiles_lon), row), device_id_type=MESH)
    for d in range(1, tiles_lat):
        pl.semaphore_signal(barrier, inc=1, device_id=(col, lax.rem(row + d, tiles_lat)), device_id_type=MESH)
    for i in range(4, 8):
        dx, dy = DIRS[i]

        @pl.when(has[i])
        def _():
            pl.semaphore_signal(barrier, inc=1, device_id=(col + dx, row + dy), device_id_type=MESH)

    q_slots = [q_e, q_w, q_n, q_s] + [q_c.at[i] for i in range(4)]
    for i, slot in enumerate(q_slots):

        @pl.when(jnp.logical_not(has[i]))
        def _():
            slot[...] = jnp.zeros(slot.shape, F32)

    l_slots = [recv_e, recv_w, recv_n, recv_s]
    for i, slot in enumerate(l_slots):

        @pl.when(jnp.logical_not(has[i]))
        def _():
            slot[...] = jnp.zeros(slot.shape, F32)

    for buf in (send_e, send_w, send_n, send_s):
        buf[...] = jnp.zeros(buf.shape, F32)

    lane = lax.broadcasted_iota(jnp.int32, (cy, cx), 1)

    def forcing_level(k, acc):
        wet = mask[k].astype(F32)
        return acc + wet * (forcing[0, k] * tracer[0, k] + forcing[1, k] * tracer[1, k])

    rhs = lax.fori_loop(0, levels, forcing_level, surface[...])
    quad[0] = rhs
    quad[1] = cond_e[...]
    quad[2] = cond_n[...]
    quad[3] = diag[...]

    n_signals = tiles_lon - 1 + tiles_lat - 1
    total = jnp.int32(n_signals)
    for i in range(4, 8):
        total = total + has[i].astype(jnp.int32)
    pl.semaphore_wait(barrier, total)

    q_src = [
        quad, quad, quad.at[:, cy - 8 : cy, :], quad.at[:, 0:8, :],
        quad.at[:, cy - 8 : cy, :], quad.at[:, cy - 8 : cy, :],
        quad.at[:, 0:8, :], quad.at[:, 0:8, :],
    ]

    def q_copy(i):
        dx, dy = DIRS[i]
        o = OPPOSITE[i]
        return pltpu.make_async_remote_copy(
            src_ref=q_src[i], dst_ref=q_slots[o], send_sem=hs.at[i], recv_sem=hr.at[o],
            device_id=(col + dx, row + dy), device_id_type=MESH)

    def q_arrival(i):
        dx, dy = DIRS[i]
        return pltpu.make_async_remote_copy(
            src_ref=q_slots[i], dst_ref=q_slots[i], send_sem=hs.at[i], recv_sem=hr.at[i],
            device_id=(col + dx, row + dy), device_id_type=MESH)

    for i in range(8):

        @pl.when(has[i])
        def _():
            q_copy(i).start()

    def forward(k, kap, carry):
        kap_prev, ratio_prev, r0, r1, r2, r3 = carry
        wet = mask[k].astype(F32)
        inv = 1.0 / (1.0 + kap + kap_prev * (1.0 - ratio_prev))
        new_ratio = kap * inv
        r0 = (tracer[0, k] + kap_prev * r0) * inv
        r1 = (tracer[1, k] + kap_prev * r1) * inv
        r2 = (wet * load[0, k] + kap_prev * r2) * inv
        r3 = (wet * load[1, k] + kap_prev * r3) * inv
        ratio[k] = new_ratio
        red[0, k] = r0
        red[1, k] = r1
        red[2, k] = r2
        red[3, k] = r3
        packed = column_roll(flow_e[k], k + 1)
        send_e[2] = jnp.where(lane == k, packed, send_e[2])
        send_n[2, pl.ds(k, 1), :] = flow_n[k, cy - 1 : cy, :]
        return kap, new_ratio, r0, r1, r2, r3

    def forward_level(k, carry):
        return forward(k, mix[k] * mask[k + 1].astype(F32), carry)

    zero = jnp.zeros((cy, cx), F32)
    carry = lax.fori_loop(0, levels - 1, forward_level, (zero,) * 6)
    forward(levels - 1, zero, carry)

    for i in range(8):

        @pl.when(has[i])
        def _():
            q_arrival(i).wait_recv()

    lane8 = lax.broadcasted_iota(jnp.int32, (8, cx), 1) < cx // 2
    sub8 = lax.broadcasted_iota(jnp.int32, (8, cx), 0) < 4
    lane_half = lane < cx // 2

    def extend(f):
        side = jnp.where(lane_half, q_e[f], q_w[f])
        ends = jnp.where(sub8, q_n[f], q_s[f])
        corner = jnp.where(
            sub8, jnp.where(lane8, q_c[0, f], q_c[1, f]), jnp.where(lane8, q_c[2, f], q_c[3, f]))
        return jnp.concatenate(
            [jnp.concatenate([quad[f], ends], axis=0), jnp.concatenate([side, corner], axis=0)], axis=1)

    v0, ce, cn, dg = extend(0), extend(1), extend(2), extend(3)
    v1 = surface_apply(v0, ce, cn, dg)
    v2 = surface_apply(v1, ce, cn, dg)
    v3 = surface_apply(v2, ce, cn, dg)
    o0, o1, o2, o3 = (v[:cy, :cx] for v in (v0, v1, v2, v3))
    pairs = ((o0, o0), (o0, o1), (o1, o1), (o1, o2), (o2, o2), (o2, o3))
    mom_send[...] = jnp.concatenate(
        [jnp.sum(a * b, axis=0, keepdims=True) for a, b in pairs] + [jnp.zeros((2, cx), F32)], axis=0)

    def along_y(d, src, dst, ssem, rsem):
        return pltpu.make_async_remote_copy(
            src_ref=src, dst_ref=dst, send_sem=ssem.at[d - 1], recv_sem=rsem.at[d - 1],
            device_id=(col, lax.rem(row + d, tiles_lat)), device_id_type=MESH)

    def along_x(d, src, dst, ssem, rsem):
        return pltpu.make_async_remote_copy(
            src_ref=src, dst_ref=dst, send_sem=ssem.at[d - 1], recv_sem=rsem.at[d - 1],
            device_id=(lax.rem(col + d, tiles_lon), row), device_id_type=MESH)

    for d in range(1, tiles_lat):
        along_y(d, mom_send, mom_y.at[d - 1], mys, myr).start()

    def backward_level(step, carry):
        k = levels - 1 - step
        c = list(carry)
        wet = mask[k].astype(F32)
        rat = ratio[k]
        for f in range(4):
            c[f] = red[f, k] + rat * c[f]
            lam = wet * c[f]
            red[f, k] = lam
            kind, s = f // 2, f % 2
            idx = s * levels + k
            packed = column_roll(lam, idx + 1)
            send_e[kind] = jnp.where(lane == idx, packed, send_e[kind])
            send_w[kind] = jnp.where(lane == idx + 1, packed, send_w[kind])
            send_s[kind, pl.ds(idx, 1), :] = lam[0:1]
            send_n[kind, pl.ds(idx, 1), :] = lam[cy - 1 : cy]
        return tuple(c)

    lax.fori_loop(0, levels, backward_level, (zero,) * 4)

    l_src = [send_e, send_w, send_n, send_s]

    def l_copy(i):
        dx, dy = DIRS[i]
        o = OPPOSITE[i]
        return pltpu.make_async_remote_copy(
            src_ref=l_src[i], dst_ref=l_slots[o], send_sem=ls.at[i], recv_sem=lr.at[o],
            device_id=(col + dx, row + dy), device_id_type=MESH)

    def l_arrival(i):
        dx, dy = DIRS[i]
        return pltpu.make_async_remote_copy(
            src_ref=l_slots[i], dst_ref=l_slots[i], send_sem=ls.at[i], recv_sem=lr.at[i],
            device_id=(col + dx, row + dy), device_id_type=MESH)

    for i in range(4):

        @pl.when(has[i])
        def _():
            l_copy(i).start()

    part = mom_send[...]
    for d in range(1, tiles_lat):
        along_y(d, mom_send, mom_y.at[d - 1], mys, myr).wait_recv()
    for d in range(1, tiles_lat):
        part = part + mom_y[d - 1]
    mom_x_send[...] = part
    for d in range(1, tiles_lon):
        along_x(d, mom_x_send, mom_x.at[d - 1], mxs, mxr).start()
    for d in range(1, tiles_lon):
        along_x(d, mom_x_send, mom_x.at[d - 1], mxs, mxr).wait_recv()
    for d in range(1, tiles_lon):
        part = part + mom_x[d - 1]
    sums = jnp.sum(part, axis=1, keepdims=True)
    w0, w1, w2 = gradient_weights([sums[i : i + 1] for i in range(6)])
    x = w0 * v0 + w1 * v1 + w2 * v2
    x_own = x[:cy, :cx]
    surf_out[...] = x_own

    for i in range(4):

        @pl.when(has[i])
        def _():
            l_arrival(i).wait_recv()

    lam_e_cols = recv_e[0] + x[:cy, cx : cx + 1] * recv_e[1]
    lam_w_cols = recv_w[0] + x[:cy, 2 * cx - 1 : 2 * cx] * recv_w[1]
    recv_n[0] = recv_n[0] + x[cy : cy + 1, :cx] * recv_n[1]
    recv_s[0] = recv_s[0] + x[cy + 7 : cy + 8, :cx] * recv_s[1]

    edge_w[...] = jnp.zeros(edge_w.shape, F32)
    edge_e[...] = jnp.zeros(edge_e.shape, F32)
    edge_s[...] = jnp.zeros(edge_s.shape, F32)
    edge_n[...] = jnp.zeros(edge_n.shape, F32)
    sub = lax.broadcasted_iota(jnp.int32, (cy, cx), 0)
    first_lane, last_lane = lane == 0, lane == cx - 1
    first_row, last_row = sub == 0, sub == cy - 1

    def final_level(k, carry):
        half_e = 0.5 * flow_e[k]
        half_n = 0.5 * flow_n[k]
        half_w_halo = 0.5 * column_roll(recv_w[2], cx - k)
        half_s_halo = 0.5 * recv_s[2, pl.ds(k, 1), :]
        for s in range(2):
            idx = s * levels + k
            lam = red[s, k] + x_own * red[2 + s, k]
            lam_e = jnp.where(last_lane, column_roll(lam_e_cols, cx - 2 - idx), column_roll(lam, cx - 1))
            lam_n = jnp.where(last_row, recv_n[0, pl.ds(idx, 1), :], pltpu.roll(lam, cy - 1, 0))
            flux_e = half_e * (lam_e - lam)
            flux_n = half_n * (lam_n - lam)
            halo_w = half_w_halo * (lam - column_roll(lam_w_cols, cx - idx))
            halo_s = half_s_halo * (lam[0:1] - recv_s[0, pl.ds(idx, 1), :])
            flux_w = jnp.where(first_lane, halo_w, column_roll(flux_e, 1))
            flux_s = jnp.where(first_row, halo_s, pltpu.roll(flux_n, 1, 0))
            g = lam + flux_e + flux_w + flux_n + flux_s
            grad_out[s, k] = g
            packed = column_roll(g, idx + 1)
            edge_e[0:cy] = jnp.where(lane == idx, packed, edge_e[0:cy])
            edge_w[0:cy] = jnp.where(lane == idx + 1, packed, edge_w[0:cy])
            edge_s[pl.ds(idx, 1), :] = g[0:1]
            edge_n[pl.ds(idx, 1), :] = g[cy - 1 : cy]
        return carry

    lax.fori_loop(0, levels, final_level, 0)

    lon, lat = tiles_lon * cx, tiles_lat * cy
    controls = ctl_send.shape[0]
    lane_row = lax.broadcasted_iota(jnp.int32, (1, LANES), 1)
    last_chunk = cmap.shape[0] - 1

    def points(ref, begin):
        chunk = begin // LANES
        off = lax.rem(begin, LANES)
        near = ref[pl.ds(chunk, 1), :]
        far = ref[pl.ds(jnp.minimum(chunk + 1, last_chunk), 1), :]
        back = lax.rem(LANES - off, LANES)
        return jnp.where(
            lane_row < LANES - off, pltpu.roll(near, back, 1), pltpu.roll(far, back, 1))

    control_ids = lax.broadcasted_iota(jnp.int32, (controls, LANES), 0)
    sides = (
        (col * cx, cx, row == 0, edge_s, True),
        (lon + col * cx, cx, row == tiles_lat - 1, edge_n, True),
        (2 * lon + row * cy, cy, col == 0, edge_w, False),
        (2 * lon + lat + row * cy, cy, col == tiles_lon - 1, edge_e, False),
    )
    ctl_send[...] = jnp.zeros(ctl_send.shape, F32)
    for begin, count, active, edge, by_rows in sides:

        @pl.when(active)
        def _():
            ids = points(cmap, begin)
            wts = jnp.where(lane_row < count, points(cwt, begin), 0.0)
            spread = jnp.where(control_ids == ids, wts, 0.0)
            values = edge[...]
            if edge is edge_w:
                values = column_roll(values, LANES - 1)
            dims = (((1,), (1,)), ((), ())) if by_rows else (((1,), (0,)), ((), ()))
            ctl_send[...] += lax.dot_general(
                spread, values, dims, precision=HIGHEST, preferred_element_type=F32)

    share = controls // tiles_lon
    for d in range(1, tiles_lon):
        begin = pl.multiple_of(lax.rem(col + d, tiles_lon) * share, 8)
        along_x(d, ctl_send.at[pl.ds(begin, share), :], ctl_x.at[d - 1], cxs, cxr).start()
    mine = ctl_send[pl.ds(pl.multiple_of(col * share, 8), share), :]
    for d in range(1, tiles_lon):
        along_x(d, ctl_send.at[pl.ds(0, share), :], ctl_x.at[d - 1], cxs, cxr).wait_recv()
    for d in range(1, tiles_lon):
        mine = mine + ctl_x[d - 1]
    ctl_y_send[...] = jnp.zeros(ctl_y_send.shape, F32)
    for j in range(tiles_lat):
        ctl_y_send[j, 0:CTRL_DEV] = mine[j * CTRL_DEV : (j + 1) * CTRL_DEV]
    for d in range(1, tiles_lat):
        along_y(d, ctl_y_send.at[lax.rem(row + d, tiles_lat)], ctl_y.at[d - 1], cys, cyr).start()
    result = ctl_y_send[row]
    for d in range(1, tiles_lat):
        along_y(d, ctl_y_send.at[0], ctl_y.at[d - 1], cys, cyr).wait_recv()
    for d in range(1, tiles_lat):
        result = result + ctl_y[d - 1]
    turned = jnp.concatenate([result, jnp.zeros((LANES - SLOT, LANES), F32)], axis=0).T
    for s in range(2):
        ctrl_out[s] = turned[s * levels : (s + 1) * levels, 0:CTRL_DEV]

    for i in range(8):

        @pl.when(has[i])
        def _():
            q_copy(i).wait_send()

    for i in range(4):

        @pl.when(has[i])
        def _():
            l_copy(i).wait_send()

    for d in range(1, tiles_lat):
        along_y(d, mom_send, mom_y.at[d - 1], mys, myr).wait_send()
        along_y(d, ctl_y_send.at[0], ctl_y.at[d - 1], cys, cyr).wait_send()
    for d in range(1, tiles_lon):
        along_x(d, mom_x_send, mom_x.at[d - 1], mxs, mxr).wait_send()
        along_x(d, ctl_send.at[pl.ds(0, share), :], ctl_x.at[d - 1], cxs, cxr).wait_send()


def per_device(
    tracer_adjoint, surface_adjoint, flow_east, flow_north, vertical_mix, land_mask,
    conduct_east, conduct_north, surface_diagonal, pressure_load, surface_forcing,
    control_map, control_weight,
):
    tiles_lon, tiles_lat = lax.axis_size("gx"), lax.axis_size("gy")
    _, levels, cy, cx = tracer_adjoint.shape
    pack = -(-2 * levels // 8) * 8
    controls = CTRL_DEV * tiles_lon * tiles_lat
    vmem = pl.BlockSpec(memory_space=pltpu.VMEM)
    smem = pl.BlockSpec(memory_space=pltpu.SMEM)
    dma = pltpu.SemaphoreType.DMA
    buf = lambda *shape: pltpu.VMEM(shape, F32)
    scratch = [
        buf(4, levels, cy, cx), buf(levels, cy, cx), buf(4, cy, cx),
        buf(4, cy, cx), buf(4, cy, cx), buf(4, 8, cx), buf(4, 8, cx), buf(4, 4, 8, cx),
        buf(3, cy, cx), buf(2, cy, cx), buf(3, pack, cx), buf(2, pack, cx),
        buf(2, cy, cx), buf(3, cy, cx), buf(2, pack, cx), buf(3, pack, cx),
        buf(8, cx), buf(tiles_lat - 1, 8, cx), buf(8, cx), buf(tiles_lon - 1, 8, cx),
        buf(LANES, cx), buf(LANES, cx), buf(LANES, cx), buf(LANES, cx),
        buf(controls, LANES), buf(tiles_lon - 1, controls // tiles_lon, LANES),
        buf(tiles_lat, SLOT, LANES), buf(tiles_lat - 1, SLOT, LANES),
        dma((8,)), dma((8,)), dma((4,)), dma((4,)),
        dma((tiles_lat - 1,)), dma((tiles_lat - 1,)), dma((tiles_lon - 1,)), dma((tiles_lon - 1,)),
        dma((tiles_lon - 1,)), dma((tiles_lon - 1,)), dma((tiles_lat - 1,)), dma((tiles_lat - 1,)),
    ]
    return pl.pallas_call(
        functools.partial(step_kernel, tiles_lon, tiles_lat, levels),
        out_shape=(
            jax.ShapeDtypeStruct(tracer_adjoint.shape, F32),
            jax.ShapeDtypeStruct(surface_adjoint.shape, F32),
            jax.ShapeDtypeStruct((2, levels, CTRL_DEV), F32),
        ),
        in_specs=[vmem] * 9 + [smem] * 2 + [vmem] * 2,
        out_specs=(vmem, vmem, vmem),
        scratch_shapes=scratch,
        compiler_params=pltpu.CompilerParams(
            collective_id=0, has_side_effects=True, vmem_limit_bytes=48 * 1024 * 1024),
    )(
        tracer_adjoint, surface_adjoint, flow_east, flow_north, vertical_mix, land_mask,
        conduct_east, conduct_north, surface_diagonal, pressure_load, surface_forcing,
        control_map.reshape(-1, LANES), control_weight.reshape(-1, LANES),
    )


def solution(mesh):
    in_specs = (
        P(None, None, "gy", "gx"), P("gy", "gx"),
        P(None, "gy", "gx"), P(None, "gy", "gx"), P(None, "gy", "gx"), P(None, "gy", "gx"),
        P("gy", "gx"), P("gy", "gx"), P("gy", "gx"), P(), P(), P(), P(),
    )
    out_specs = (P(None, None, "gy", "gx"), P("gy", "gx"), P(None, None, ("gx", "gy")))
    return jax.shard_map(
        per_device, mesh=mesh, in_specs=in_specs, out_specs=out_specs, check_vma=False
    )
```

time: 543 us -> 60.2 us (0.11)
  blocking collectives: 209 us -> 0 us
  waiting for transfers between devices: 129 us -> 0 us
  other arithmetic: 78.5 us -> 0 us
  starting transfers between devices: 51.1 us -> 0 us
  Pallas kernels: 0 us -> 44 us
  local copies, waits for them, and re-layouts: 48.2 us -> 14.8 us
  between operations: 22.9 us -> 0.66 us
    psum x5 -> x0, blocking collectives: 209 us -> none  [the longest x3 123 us: squares(): return lax.psum(jnp.sum(remain * remain), ('gx', 'gy'))]
    psum x1 -> x0, waiting for transfers between devices: 125 us -> none  [per_device(): totals = lax.psum(contribution, ('gx', 'gy'))]
    ppermute x18 -> x0, starting transfers between devices: 51 us -> none  [the longest x8 32.3 us: extended(): before = lax.ppermute(last, axis, up)]
    pallas_call x0 -> x1, Pallas kernels: none -> 44 us  [per_device(): pl.pallas_call(functools.partial(step_kernel, tiles_lon, tiles_lat, level...]
    slice x13 -> x0, local copies, waits for them, and re-layouts: 25.3 us -> none  [the longest x5 8.72 us: extended(): last = lax.slice_in_dim(shard, length - width, length, axis=dim)]
    mul x30 -> x0, other arithmetic: 24 us -> none  [the longest x21 15.3 us: column_solve(): solution.insert(0, reduced[level] + ratios[level] * solution[0])]
    add x6 -> x0, other arithmetic: 17.1 us -> none  [the longest x1 13 us: per_device(): center + 0.5 * flow_east * (east_side - center)]
    div x3 -> x0, other arithmetic: 11.8 us -> none  [column_solve(): reduced.append(carried / pivot_val)]
  transfers between devices with their start and end apart: 19 -> 0, of which waited for: 4 -> 0; matrix products, arithmetic and copies ran while one was open for 9% -> 0% of each run, Pallas kernels for 0% -> 0%
where the time goes in v1:
time: 60.2 us; the launch traced here: 59.5 us
  Pallas kernels  44 us (73%)
  local copies, waits for them, and re-layouts  14.8 us (25%)
  between operations  0.66 us (1%)
    pallas_call x1, Pallas kernels, per_device(): pl.pallas_call(functools.partial(step_kernel, tiles_lon, tiles_lat, level...  44 us
    unnamed x26, local copies, waits for them, and re-layouts  14.1 us

profile of v1, /device:TPU:0, one launch (start us, length us, event | category | flops | bytes accessed | tf_op | source)
XLA Modules:
  0.0 59.5 jit_solution(12925127387971028283)
XLA Ops:
  0.6 0.0 copy-start
  0.6 1.2 %copy-done = f32[50,40,128]{2,1,0:T(8,128)S(1)} copy-done((f32[50,40,128]{2,1,0:T(8,128)S(1)}, f32[50,40,128]{2,1,0:T(8,128)}, u32[]{:S(2)}) %copy-start) | copy-done | bytes 1024024
  1.9 0.0 copy-start.1
  1.9 1.2 %copy-done.1 = f32[50,40,128]{2,1,0:T(8,128)S(1)} copy-done((f32[50,40,128]{2,1,0:T(8,128)S(1)}, f32[50,40,128]{2,1,0:T(8,128)}, u32[]{:S(2)}) %copy-start.1) | copy-done | bytes 1024024
  3.1 0.0 copy-start.2
  3.1 1.2 %copy-done.2 = s32[50,40,128]{2,1,0:T(8,128)S(1)} copy-done((s32[50,40,128]{2,1,0:T(8,128)S(1)}, s32[50,40,128]{2,1,0:T(8,128)}, u32[]{:S(2)}) %copy-start.2) | copy-done | bytes 1024024
  4.3 0.0 copy-start.3
  4.3 1.2 %copy-done.3 = f32[49,40,128]{2,1,0:T(8,128)S(1)} copy-done((f32[49,40,128]{2,1,0:T(8,128)S(1)}, f32[49,40,128]{2,1,0:T(8,128)}, u32[]{:S(2)}) %copy-start.3) | copy-done | bytes 1003544
  5.5 0.0 copy-start.4
  5.5 0.7 %copy-done.4 = f32[40,128]{1,0:T(8,128)S(1)} copy-done((f32[40,128]{1,0:T(8,128)S(1)}, f32[40,128]{1,0:T(8,128)}, u32[]{:S(2)}) %copy-start.4) | copy-done | bytes 20504
  6.2 0.0 copy-start.5
  6.2 0.7 %copy-done.5 = f32[40,128]{1,0:T(8,128)S(1)} copy-done((f32[40,128]{1,0:T(8,128)S(1)}, f32[40,128]{1,0:T(8,128)}, u32[]{:S(2)}) %copy-start.5) | copy-done | bytes 20504
  7.0 0.0 copy-start.6
  7.0 0.7 %copy-done.6 = f32[40,128]{1,0:T(8,128)S(1)} copy-done((f32[40,128]{1,0:T(8,128)S(1)}, f32[40,128]{1,0:T(8,128)}, u32[]{:S(2)}) %copy-start.6) | copy-done | bytes 20504
  7.7 0.0 copy-start.7
  7.7 0.7 %copy-done.7 = f32[40,128]{1,0:T(8,128)S(1)} copy-done((f32[40,128]{1,0:T(8,128)S(1)}, f32[40,128]{1,0:T(8,128)}, u32[]{:S(2)}) %copy-start.7) | copy-done | bytes 20504
  8.4 0.0 copy-start.8
  8.4 0.7 %copy-done.8 = s32[1664]{0:T(1024)S(1)} copy-done((s32[1664]{0:T(1024)S(1)}, s32[1664]{0:T(1024)}, u32[]{:S(2)}) %copy-start.8) | copy-done | bytes 6680
  9.1 0.0 copy-start.9
  9.1 0.7 %copy-done.9 = f32[1664]{0:T(1024)S(1)} copy-done((f32[1664]{0:T(1024)S(1)}, f32[1664]{0:T(1024)}, u32[]{:S(2)}) %copy-start.9) | copy-done | bytes 6680
  9.8 0.0 copy-start.10
  9.8 0.7 %copy-done.10 = f32[2,50]{1,0:T(2,128)S(1)} copy-done((f32[2,50]{1,0:T(2,128)S(1)}, f32[2,50]{1,0:T(2,128)}, u32[]{:S(2)}) %copy-start.10) | copy-done | bytes 424
  10.5 0.0 copy-start.11
  10.5 0.7 %copy-done.11 = f32[2,50]{1,0:T(2,128)S(1)} copy-done((f32[2,50]{1,0:T(2,128)S(1)}, f32[2,50]{1,0:T(2,128)}, u32[]{:S(2)}) %copy-start.11) | copy-done | bytes 424
  11.2 44.0 %shard_map.148 = (f32[2,50,40,128]{3,2,1,0:T(8,128)}, f32[40,128]{1,0:T(8,128)S(1)}, f32[2,50,10]{2,1,0:T(8,128)S(1)}) custom-call(f32[2,50,40,128]{3,2,1,0:T(8,128)} %tracer.1, f32[40,128]{1,0:T(8,128)S(1)} %copy-done.4, f32[50,40,128]{2,1,0:T(8,128)S(1)} %copy-done, f32[50,40,128]{2,1,0:T(8,128)S(1)} %copy-done.1, f32[49,40,128]{2,1,0:T(8,128)S(1)} %copy-done.3, ...), custom_call_target="tpu_custom_call" | custom-call | tf_op jit(solution)/shard_map/pallas_call | solution.py:442
  55.2 0.7 %copy.16 = f32[2,50,10]{1,0,2:T(2,128)} copy(f32[2,50,10]{2,1,0:T(8,128)S(1)} %get-tuple-element.5) | data formatting | bytes 8000 | tf_op jit(solution)/shard_map/pallas_call | solution.py:442
  55.9 3.0 %copy.19 = f32[2,50,40,128]{3,2,1,0:T(8,128)} copy(f32[2,50,40,128]{3,2,1,0:T(8,128)} %get-tuple-element.9) | data formatting | bytes 4096000
  58.9 0.6 %copy.20 = f32[40,128]{1,0:T(8,128)} copy(f32[40,128]{1,0:T(8,128)S(1)} %get-tuple-element.10) | data formatting | bytes 40960
Async XLA Ops:
  0.6 1.2 %copy-start = (f32[50,40,128]{2,1,0:T(8,128)S(1)}, f32[50,40,128]{2,1,0:T(8,128)}, u32[]{:S(2)}) copy-start(f32[50,40,128]{2,1,0:T(8,128)} %flow_e.1) | copy-start | bytes 3072004
  1.9 1.2 %copy-start.1 = (f32[50,40,128]{2,1,0:T(8,128)S(1)}, f32[50,40,128]{2,1,0:T(8,128)}, u32[]{:S(2)}) copy-start(f32[50,40,128]{2,1,0:T(8,128)} %flow_n.1) | copy-start | bytes 3072004
  3.1 1.2 %copy-start.2 = (s32[50,40,128]{2,1,0:T(8,128)S(1)}, s32[50,40,128]{2,1,0:T(8,128)}, u32[]{:S(2)}) copy-start(s32[50,40,128]{2,1,0:T(8,128)} %mask.1) | copy-start | bytes 3072004
  4.3 1.2 %copy-start.3 = (f32[49,40,128]{2,1,0:T(8,128)S(1)}, f32[49,40,128]{2,1,0:T(8,128)}, u32[]{:S(2)}) copy-start(f32[49,40,128]{2,1,0:T(8,128)} %mix.1) | copy-start | bytes 3010564
  5.5 0.7 %copy-start.4 = (f32[40,128]{1,0:T(8,128)S(1)}, f32[40,128]{1,0:T(8,128)}, u32[]{:S(2)}) copy-start(f32[40,128]{1,0:T(8,128)} %surface.1) | copy-start | bytes 61444
  6.2 0.7 %copy-start.5 = (f32[40,128]{1,0:T(8,128)S(1)}, f32[40,128]{1,0:T(8,128)}, u32[]{:S(2)}) copy-start(f32[40,128]{1,0:T(8,128)} %cond_e.1) | copy-start | bytes 61444
  7.0 0.7 %copy-start.6 = (f32[40,128]{1,0:T(8,128)S(1)}, f32[40,128]{1,0:T(8,128)}, u32[]{:S(2)}) copy-start(f32[40,128]{1,0:T(8,128)} %cond_n.1) | copy-start | bytes 61444
  7.7 0.7 %copy-start.7 = (f32[40,128]{1,0:T(8,128)S(1)}, f32[40,128]{1,0:T(8,128)}, u32[]{:S(2)}) copy-start(f32[40,128]{1,0:T(8,128)} %diag.1) | copy-start | bytes 61444
  8.4 0.7 %copy-start.8 = (s32[1664]{0:T(1024)S(1)}, s32[1664]{0:T(1024)}, u32[]{:S(2)}) copy-start(s32[1664]{0:T(1024)} %param.24) | copy-start | bytes 19972
  9.1 0.7 %copy-start.9 = (f32[1664]{0:T(1024)S(1)}, f32[1664]{0:T(1024)}, u32[]{:S(2)}) copy-start(f32[1664]{0:T(1024)} %param.25) | copy-start | bytes 19972
  9.8 0.7 %copy-start.10 = (f32[2,50]{1,0:T(2,128)S(1)}, f32[2,50]{1,0:T(2,128)}, u32[]{:S(2)}) copy-start(f32[2,50]{1,0:T(2,128)} %load.1) | copy-start | bytes 1204
  10.5 0.7 %copy-start.11 = (f32[2,50]{1,0:T(2,128)S(1)}, f32[2,50]{1,0:T(2,128)}, u32[]{:S(2)}) copy-start(f32[2,50]{1,0:T(2,128)} %forcing.1) | copy-start | bytes 1204

commit v2 on v1

--- a/solution.py
+++ b/solution.py
@@ -9,12 +9,24 @@
 ITERS = 3
 CTRL_DEV = 10
 SLOT = 16
+VMEM_LIMIT = 63_200 * 1024
 LANES = 128
 MESH = pl.DeviceIdType.MESH
 DIRS = ((1, 0), (-1, 0), (0, 1), (0, -1), (1, 1), (-1, 1), (1, -1), (-1, -1))
 OPPOSITE = (1, 0, 3, 2, 7, 6, 5, 4)
 F32 = jnp.float32
 HIGHEST = lax.Precision.HIGHEST
+
+
+def unrolled(count, body, carry):
+    width = max(u for u in range(1, 8) if count % u == 0)
+
+    def several(i, carry):
+        for u in range(width):
+            carry = body(i * width + u, carry)
+        return carry
+
+    return lax.fori_loop(0, count // width, several, carry)
 
 
 def column_roll(value, shift):
@@ -69,19 +81,30 @@
 
 def step_kernel(
     tiles_lon, tiles_lat, levels,
-    tracer, surface, flow_e, flow_n, mix, mask, cond_e, cond_n, diag, load, forcing, cmap, cwt,
+    tracer_in, surface_in, flow_e_in, flow_n_in, mix_in, mask_in, cond_e_in, cond_n_in, diag_in,
+    load_in, forcing_in, cmap_in, cwt_in,
     grad_out, surf_out, ctrl_out,
+    tracer, surface, flow_e, flow_n, mix, mask, load, forcing, cmap, cwt, ins,
     red, ratio, quad, q_e, q_w, q_n, q_s, q_c,
-    send_e, send_w, send_n, send_s, recv_e, recv_w, recv_n, recv_s,
+    pk, send_n, send_s, recv_e, recv_w, recv_n, recv_s,
     mom_send, mom_y, mom_x_send, mom_x,
-    edge_s, edge_n, edge_w, edge_e,
+    edge_s, edge_n, edge_ew,
     ctl_send, ctl_x, ctl_y_send, ctl_y,
     hs, hr, ls, lr, mys, myr, mxs, mxr, cxs, cxr, cys, cyr,
 ):
     col = lax.axis_index("gx")
     row = lax.axis_index("gy")
     cy, cx = surface.shape
-    pack = edge_s.shape[0]
+    moves = [
+        pltpu.make_async_copy(src, dst, ins.at[i])
+        for i, (src, dst) in enumerate((
+            (forcing_in, forcing), (mask_in, mask), (tracer_in, tracer), (surface_in, surface),
+            (cond_e_in, quad.at[1]), (cond_n_in, quad.at[2]), (diag_in, quad.at[3]),
+            (load_in, load), (mix_in, mix), (flow_e_in, flow_e), (flow_n_in, flow_n),
+            (cmap_in, cmap), (cwt_in, cwt)))
+    ]
+    for move in moves:
+        move.start()
     has = []
     for dx, dy in DIRS:
         ok = None
@@ -117,8 +140,11 @@
         def _():
             slot[...] = jnp.zeros(slot.shape, F32)
 
-    for buf in (send_e, send_w, send_n, send_s):
+    for buf in (pk, send_n, send_s, edge_s, edge_n, edge_ew):
         buf[...] = jnp.zeros(buf.shape, F32)
+
+    for move in moves[:4]:
+        move.wait()
 
     lane = lax.broadcasted_iota(jnp.int32, (cy, cx), 1)
 
@@ -126,11 +152,9 @@
         wet = mask[k].astype(F32)
         return acc + wet * (forcing[0, k] * tracer[0, k] + forcing[1, k] * tracer[1, k])
 
-    rhs = lax.fori_loop(0, levels, forcing_level, surface[...])
-    quad[0] = rhs
-    quad[1] = cond_e[...]
-    quad[2] = cond_n[...]
-    quad[3] = diag[...]
+    quad[0] = unrolled(levels, forcing_level, surface[...])
+    for move in moves[4:7]:
+        move.wait()
 
     n_signals = tiles_lon - 1 + tiles_lat - 1
     total = jnp.int32(n_signals)
@@ -177,16 +201,18 @@
         red[1, k] = r1
         red[2, k] = r2
         red[3, k] = r3
-        packed = column_roll(flow_e[k], k + 1)
-        send_e[2] = jnp.where(lane == k, packed, send_e[2])
+        pk[4] = jnp.where(pair == k, column_roll(flow_e[k], 2 * k + 1), pk[4])
         send_n[2, pl.ds(k, 1), :] = flow_n[k, cy - 1 : cy, :]
         return kap, new_ratio, r0, r1, r2, r3
 
     def forward_level(k, carry):
         return forward(k, mix[k] * mask[k + 1].astype(F32), carry)
 
+    for move in moves[7:11]:
+        move.wait()
+    pair = lane // 2
     zero = jnp.zeros((cy, cx), F32)
-    carry = lax.fori_loop(0, levels - 1, forward_level, (zero,) * 6)
+    carry = unrolled(levels - 1, forward_level, (zero,) * 6)
     forward(levels - 1, zero, carry)
 
     for i in range(8):
@@ -240,16 +266,14 @@
             red[f, k] = lam
             kind, s = f // 2, f % 2
             idx = s * levels + k
-            packed = column_roll(lam, idx + 1)
-            send_e[kind] = jnp.where(lane == idx, packed, send_e[kind])
-            send_w[kind] = jnp.where(lane == idx + 1, packed, send_w[kind])
+            pk[f] = jnp.where(pair == k, column_roll(lam, 2 * k + 1), pk[f])
             send_s[kind, pl.ds(idx, 1), :] = lam[0:1]
             send_n[kind, pl.ds(idx, 1), :] = lam[cy - 1 : cy]
         return tuple(c)
 
-    lax.fori_loop(0, levels, backward_level, (zero,) * 4)
-
-    l_src = [send_e, send_w, send_n, send_s]
+    unrolled(levels, backward_level, (zero,) * 4)
+
+    l_src = [pk, pk.at[0:4], send_n, send_s]
 
     def l_copy(i):
         dx, dy = DIRS[i]
@@ -294,15 +318,16 @@
         def _():
             l_arrival(i).wait_recv()
 
-    lam_e_cols = recv_e[0] + x[:cy, cx : cx + 1] * recv_e[1]
-    lam_w_cols = recv_w[0] + x[:cy, 2 * cx - 1 : 2 * cx] * recv_w[1]
+    even = lane == 2 * pair
+    x_e, x_w = x[:cy, cx : cx + 1], x[:cy, 2 * cx - 1 : 2 * cx]
+    for s in range(2):
+        recv_e[s] = jnp.where(
+            even,
+            column_roll(recv_e[s] + x_e * recv_e[2 + s], cx - 1),
+            column_roll(recv_w[s] + x_w * recv_w[2 + s], 1))
     recv_n[0] = recv_n[0] + x[cy : cy + 1, :cx] * recv_n[1]
     recv_s[0] = recv_s[0] + x[cy + 7 : cy + 8, :cx] * recv_s[1]
 
-    edge_w[...] = jnp.zeros(edge_w.shape, F32)
-    edge_e[...] = jnp.zeros(edge_e.shape, F32)
-    edge_s[...] = jnp.zeros(edge_s.shape, F32)
-    edge_n[...] = jnp.zeros(edge_n.shape, F32)
     sub = lax.broadcasted_iota(jnp.int32, (cy, cx), 0)
     first_lane, last_lane = lane == 0, lane == cx - 1
     first_row, last_row = sub == 0, sub == cy - 1
@@ -310,29 +335,30 @@
     def final_level(k, carry):
         half_e = 0.5 * flow_e[k]
         half_n = 0.5 * flow_n[k]
-        half_w_halo = 0.5 * column_roll(recv_w[2], cx - k)
+        half_w_halo = 0.5 * column_roll(recv_w[4], lax.rem(cx - 2 * k, cx))
         half_s_halo = 0.5 * recv_s[2, pl.ds(k, 1), :]
         for s in range(2):
             idx = s * levels + k
             lam = red[s, k] + x_own * red[2 + s, k]
-            lam_e = jnp.where(last_lane, column_roll(lam_e_cols, cx - 2 - idx), column_roll(lam, cx - 1))
+            side = column_roll(recv_e[s], cx - 1 - 2 * k)
+            lam_e = jnp.where(last_lane, side, column_roll(lam, cx - 1))
             lam_n = jnp.where(last_row, recv_n[0, pl.ds(idx, 1), :], pltpu.roll(lam, cy - 1, 0))
             flux_e = half_e * (lam_e - lam)
             flux_n = half_n * (lam_n - lam)
-            halo_w = half_w_halo * (lam - column_roll(lam_w_cols, cx - idx))
+            halo_w = half_w_halo * (lam - side)
             halo_s = half_s_halo * (lam[0:1] - recv_s[0, pl.ds(idx, 1), :])
             flux_w = jnp.where(first_lane, halo_w, column_roll(flux_e, 1))
             flux_s = jnp.where(first_row, halo_s, pltpu.roll(flux_n, 1, 0))
             g = lam + flux_e + flux_w + flux_n + flux_s
             grad_out[s, k] = g
-            packed = column_roll(g, idx + 1)
-            edge_e[0:cy] = jnp.where(lane == idx, packed, edge_e[0:cy])
-            edge_w[0:cy] = jnp.where(lane == idx + 1, packed, edge_w[0:cy])
+            edge_ew[s] = jnp.where(pair == k, column_roll(g, 2 * k + 1), edge_ew[s])
             edge_s[pl.ds(idx, 1), :] = g[0:1]
             edge_n[pl.ds(idx, 1), :] = g[cy - 1 : cy]
         return carry
 
-    lax.fori_loop(0, levels, final_level, 0)
+    unrolled(levels, final_level, 0)
+    for move in moves[11:]:
+        move.wait()
 
     lon, lat = tiles_lon * cx, tiles_lat * cy
     controls = ctl_send.shape[0]
@@ -350,23 +376,32 @@
 
     control_ids = lax.broadcasted_iota(jnp.int32, (controls, LANES), 0)
     sides = (
-        (col * cx, cx, row == 0, edge_s, True),
-        (lon + col * cx, cx, row == tiles_lat - 1, edge_n, True),
-        (2 * lon + row * cy, cy, col == 0, edge_w, False),
-        (2 * lon + lat + row * cy, cy, col == tiles_lon - 1, edge_e, False),
+        (col * cx, cx, row == 0, edge_s, None),
+        (lon + col * cx, cx, row == tiles_lat - 1, edge_n, None),
+        (2 * lon + row * cy, cy, col == 0, edge_ew, 1),
+        (2 * lon + lat + row * cy, cy, col == tiles_lon - 1, edge_ew, 0),
     )
     ctl_send[...] = jnp.zeros(ctl_send.shape, F32)
-    for begin, count, active, edge, by_rows in sides:
+    for begin, count, active, edge, odd in sides:
 
         @pl.when(active)
         def _():
             ids = points(cmap, begin)
             wts = jnp.where(lane_row < count, points(cwt, begin), 0.0)
             spread = jnp.where(control_ids == ids, wts, 0.0)
-            values = edge[...]
-            if edge is edge_w:
-                values = column_roll(values, LANES - 1)
-            dims = (((1,), (1,)), ((), ())) if by_rows else (((1,), (0,)), ((), ()))
+            if odd is None:
+                values, dims = edge[...], (((1,), (1,)), ((), ()))
+            else:
+                source = lax.broadcasted_iota(jnp.int32, (LANES, LANES), 0)
+                target = lax.broadcasted_iota(jnp.int32, (LANES, LANES), 1)
+                values, dims = jnp.zeros((cy, LANES), F32), (((1,), (0,)), ((), ()))
+                for s in range(2):
+                    level = target - s * levels
+                    move = (source == 2 * level + odd) & (level >= 0) & (level < levels)
+                    values += lax.dot_general(
+                        edge[s], move.astype(F32), dims, precision=HIGHEST,
+                        preferred_element_type=F32)
+                spread = spread[:, :cy]
             ctl_send[...] += lax.dot_general(
                 spread, values, dims, precision=HIGHEST, preferred_element_type=F32)
 
@@ -389,9 +424,8 @@
         along_y(d, ctl_y_send.at[0], ctl_y.at[d - 1], cys, cyr).wait_recv()
     for d in range(1, tiles_lat):
         result = result + ctl_y[d - 1]
-    turned = jnp.concatenate([result, jnp.zeros((LANES - SLOT, LANES), F32)], axis=0).T
     for s in range(2):
-        ctrl_out[s] = turned[s * levels : (s + 1) * levels, 0:CTRL_DEV]
+        ctrl_out[:, s, :] = result[0:CTRL_DEV, s * levels : (s + 1) * levels]
 
     for i in range(8):
 
@@ -411,6 +445,17 @@
     for d in range(1, tiles_lon):
         along_x(d, mom_x_send, mom_x.at[d - 1], mxs, mxr).wait_send()
         along_x(d, ctl_send.at[pl.ds(0, share), :], ctl_x.at[d - 1], cxs, cxr).wait_send()
+
+
+def results_kernel(grad, surf, ctrl, grad_out, surf_out, ctrl_out, sems):
+    moves = [
+        pltpu.make_async_copy(src, dst, sems.at[i])
+        for i, (src, dst) in enumerate(((grad, grad_out), (surf, surf_out), (ctrl, ctrl_out)))
+    ]
+    for move in moves:
+        move.start()
+    for move in moves:
+        move.wait()
 
 
 def per_device(
@@ -422,40 +467,53 @@
     _, levels, cy, cx = tracer_adjoint.shape
     pack = -(-2 * levels // 8) * 8
     controls = CTRL_DEV * tiles_lon * tiles_lat
+    points = control_map.shape[0]
     vmem = pl.BlockSpec(memory_space=pltpu.VMEM)
-    smem = pl.BlockSpec(memory_space=pltpu.SMEM)
+    hbm = pl.BlockSpec(memory_space=pltpu.HBM)
     dma = pltpu.SemaphoreType.DMA
     buf = lambda *shape: pltpu.VMEM(shape, F32)
     scratch = [
+        buf(2, levels, cy, cx), buf(cy, cx), buf(levels, cy, cx), buf(levels, cy, cx),
+        buf(levels - 1, cy, cx), pltpu.VMEM((levels, cy, cx), jnp.int32),
+        pltpu.SMEM((2, levels), F32), pltpu.SMEM((2, levels), F32),
+        pltpu.VMEM((points // LANES, LANES), jnp.int32), buf(points // LANES, LANES), dma((13,)),
         buf(4, levels, cy, cx), buf(levels, cy, cx), buf(4, cy, cx),
         buf(4, cy, cx), buf(4, cy, cx), buf(4, 8, cx), buf(4, 8, cx), buf(4, 4, 8, cx),
-        buf(3, cy, cx), buf(2, cy, cx), buf(3, pack, cx), buf(2, pack, cx),
-        buf(2, cy, cx), buf(3, cy, cx), buf(2, pack, cx), buf(3, pack, cx),
+        buf(5, cy, cx), buf(3, pack, cx), buf(2, pack, cx),
+        buf(4, cy, cx), buf(5, cy, cx), buf(2, pack, cx), buf(3, pack, cx),
         buf(8, cx), buf(tiles_lat - 1, 8, cx), buf(8, cx), buf(tiles_lon - 1, 8, cx),
-        buf(LANES, cx), buf(LANES, cx), buf(LANES, cx), buf(LANES, cx),
+        buf(LANES, cx), buf(LANES, cx), buf(2, cy, cx),
         buf(controls, LANES), buf(tiles_lon - 1, controls // tiles_lon, LANES),
         buf(tiles_lat, SLOT, LANES), buf(tiles_lat - 1, SLOT, LANES),
         dma((8,)), dma((8,)), dma((4,)), dma((4,)),
         dma((tiles_lat - 1,)), dma((tiles_lat - 1,)), dma((tiles_lon - 1,)), dma((tiles_lon - 1,)),
         dma((tiles_lon - 1,)), dma((tiles_lon - 1,)), dma((tiles_lat - 1,)), dma((tiles_lat - 1,)),
     ]
-    return pl.pallas_call(
+    grad, surf, ctrl = pl.pallas_call(
         functools.partial(step_kernel, tiles_lon, tiles_lat, levels),
         out_shape=(
-            jax.ShapeDtypeStruct(tracer_adjoint.shape, F32),
-            jax.ShapeDtypeStruct(surface_adjoint.shape, F32),
-            jax.ShapeDtypeStruct((2, levels, CTRL_DEV), F32),
+            pltpu.VMEM(tracer_adjoint.shape, F32),
+            pltpu.VMEM(surface_adjoint.shape, F32),
+            pltpu.VMEM((CTRL_DEV, 2, levels), F32),
         ),
-        in_specs=[vmem] * 9 + [smem] * 2 + [vmem] * 2,
+        in_specs=[hbm] * 13,
         out_specs=(vmem, vmem, vmem),
         scratch_shapes=scratch,
         compiler_params=pltpu.CompilerParams(
-            collective_id=0, has_side_effects=True, vmem_limit_bytes=48 * 1024 * 1024),
+            collective_id=0, has_side_effects=True, vmem_limit_bytes=VMEM_LIMIT),
     )(
         tracer_adjoint, surface_adjoint, flow_east, flow_north, vertical_mix, land_mask,
         conduct_east, conduct_north, surface_diagonal, pressure_load, surface_forcing,
         control_map.reshape(-1, LANES), control_weight.reshape(-1, LANES),
     )
+    grad, surf, ctrl = pl.pallas_call(
+        results_kernel,
+        out_shape=tuple(jax.ShapeDtypeStruct(a.shape, F32) for a in (grad, surf, ctrl)),
+        in_specs=[vmem] * 3,
+        out_specs=(hbm, hbm, hbm),
+        scratch_shapes=[dma((3,))],
+    )(grad, surf, ctrl)
+    return grad, surf, ctrl.transpose(1, 2, 0)
 
 
 def solution(mesh):

time: 60.2 us -> 38.7 us (0.64)
  local copies, waits for them, and re-layouts: 14.8 us -> 2.51 us
  Pallas kernels: 44 us -> 35.4 us
    unnamed x26 -> x6, local copies, waits for them, and re-layouts: 14.1 us -> 2.51 us
    pallas_call x1, Pallas kernels: 44 us -> 32.5 us  [per_device(): pl.pallas_call(functools.partial(step_kernel, tiles_lon, tiles_lat, level...]
    pallas_call x0 -> x1, Pallas kernels: none -> 2.92 us  [per_device(): pl.pallas_call(results_kernel, out_shape=tuple((jax.ShapeDtypeStruct(a.sh...]
    pallas_call x1 -> x0, local copies, waits for them, and re-layouts: 0.69 us -> none  [per_device(): pl.pallas_call(functools.partial(step_kernel, tiles_lon, tiles_lat, level...]
where the time goes in v2:
time: 38.7 us; the launch traced here: 38.5 us
  Pallas kernels  35.4 us (91%)
  local copies, waits for them, and re-layouts  2.51 us (6%)
  between operations  0.65 us (2%)
    pallas_call x1, Pallas kernels, per_device(): pl.pallas_call(functools.partial(step_kernel, tiles_lon, tiles_lat, level...  32.5 us
    pallas_call x1, Pallas kernels, per_device(): pl.pallas_call(results_kernel, out_shape=tuple((jax.ShapeDtypeStruct(a.sh...  2.92 us
    unnamed x6, local copies, waits for them, and re-layouts  2.51 us

profile of v2, /device:TPU:0, one launch (start us, length us, event | category | flops | bytes accessed | tf_op | source)
XLA Modules:
  0.0 38.5 jit_solution(2821134309690505944)
XLA Ops:
  0.6 32.5 %shard_map.148 = (f32[2,50,40,128]{3,2,1,0:T(8,128)S(1)}, f32[40,128]{1,0:T(8,128)S(1)}, f32[10,2,50]{2,1,0:T(2,128)S(1)}) custom-call(f32[2,50,40,128]{3,2,1,0:T(8,128)} %tracer_in.1, f32[40,128]{1,0:T(8,128)} %surface_in.1, f32[50,40,128]{2,1,0:T(8,128)} %flow_e_in.1, f32[50,40,128]{2,1,0:T(8,128)} %flow_n_in.1, f32[49,40,128]{2,1,0:T(8,128)} %mix_in.1, ...), custom_call_target="tpu_custom_call" | custom-call | tf_op jit(solution)/shard_map/pallas_call | solution.py:492
  33.1 0.0 copy-start
  33.1 1.3 %copy-done = f32[2,50,40,128]{3,2,1,0:T(8,128)} copy-done((f32[2,50,40,128]{3,2,1,0:T(8,128)}, f32[2,50,40,128]{3,2,1,0:T(8,128)S(1)}, u32[]{:S(2)}) %copy-start) | copy-done | bytes 2048024
  34.4 0.0 copy-start.1
  34.4 0.6 %copy-done.1 = f32[40,128]{1,0:T(8,128)} copy-done((f32[40,128]{1,0:T(8,128)}, f32[40,128]{1,0:T(8,128)S(1)}, u32[]{:S(2)}) %copy-start.1) | copy-done | bytes 20504
  35.0 0.0 copy-start.2
  35.0 0.6 %copy-done.2 = f32[10,2,50]{2,1,0:T(2,128)} copy-done((f32[10,2,50]{2,1,0:T(2,128)}, f32[10,2,50]{2,1,0:T(2,128)S(1)}, u32[]{:S(2)}) %copy-start.2) | copy-done | bytes 4024
  35.6 2.9 %shard_map.149 = (f32[2,50,40,128]{3,2,1,0:T(8,128)}, f32[40,128]{1,0:T(8,128)}, f32[10,2,50]{2,1,0:T(2,128)}) custom-call(f32[2,50,40,128]{3,2,1,0:T(8,128)} %copy-done, f32[40,128]{1,0:T(8,128)} %copy-done.1, f32[10,2,50]{2,1,0:T(2,128)} %copy-done.2), custom_call_target="tpu_custom_call" | custom-call | tf_op jit(solution)/shard_map/pallas_call | solution.py:509
Async XLA Ops:
  33.1 1.3 %copy-start = (f32[2,50,40,128]{3,2,1,0:T(8,128)}, f32[2,50,40,128]{3,2,1,0:T(8,128)S(1)}, u32[]{:S(2)}) copy-start(f32[2,50,40,128]{3,2,1,0:T(8,128)S(1)} %get-tuple-element.9.grad) | copy-start | bytes 6144004
  34.4 0.6 %copy-start.1 = (f32[40,128]{1,0:T(8,128)}, f32[40,128]{1,0:T(8,128)S(1)}, u32[]{:S(2)}) copy-start(f32[40,128]{1,0:T(8,128)S(1)} %get-tuple-element.10.surf) | copy-start | bytes 61444
  35.0 0.6 %copy-start.2 = (f32[10,2,50]{2,1,0:T(2,128)}, f32[10,2,50]{2,1,0:T(2,128)S(1)}, u32[]{:S(2)}) copy-start(f32[10,2,50]{2,1,0:T(2,128)S(1)} %get-tuple-element.11.ctrl) | copy-start | bytes 12004

commit v3 on v2

--- a/solution.py
+++ b/solution.py
@@ -88,7 +88,7 @@
     red, ratio, quad, q_e, q_w, q_n, q_s, q_c,
     pk, send_n, send_s, recv_e, recv_w, recv_n, recv_s,
     mom_send, mom_y, mom_x_send, mom_x,
-    edge_s, edge_n, edge_ew,
+    edge_s, edge_n, edge_ew, parts,
     ctl_send, ctl_x, ctl_y_send, ctl_y,
     hs, hr, ls, lr, mys, myr, mxs, mxr, cxs, cxr, cys, cyr,
 ):
@@ -105,6 +105,7 @@
     ]
     for move in moves:
         move.start()
+
     has = []
     for dx, dy in DIRS:
         ok = None
@@ -255,8 +256,8 @@
     for d in range(1, tiles_lat):
         along_y(d, mom_send, mom_y.at[d - 1], mys, myr).start()
 
-    def backward_level(step, carry):
-        k = levels - 1 - step
+    def backward_level(first, step, carry):
+        k = levels - 1 - first - step
         c = list(carry)
         wet = mask[k].astype(F32)
         rat = ratio[k]
@@ -271,7 +272,17 @@
             send_n[kind, pl.ds(idx, 1), :] = lam[cy - 1 : cy]
         return tuple(c)
 
-    unrolled(levels, backward_level, (zero,) * 4)
+    early = levels // 2
+    lower = unrolled(early, functools.partial(backward_level, 0), (zero,) * 4)
+    part = mom_send[...]
+    for d in range(1, tiles_lat):
+        along_y(d, mom_send, mom_y.at[d - 1], mys, myr).wait_recv()
+    for d in range(1, tiles_lat):
+        part = part + mom_y[d - 1]
+    mom_x_send[...] = part
+    for d in range(1, tiles_lon):
+        along_x(d, mom_x_send, mom_x.at[d - 1], mxs, mxr).start()
+    unrolled(levels - early, functools.partial(backward_level, early), lower)
 
     l_src = [pk, pk.at[0:4], send_n, send_s]
 
@@ -294,14 +305,6 @@
         def _():
             l_copy(i).start()
 
-    part = mom_send[...]
-    for d in range(1, tiles_lat):
-        along_y(d, mom_send, mom_y.at[d - 1], mys, myr).wait_recv()
-    for d in range(1, tiles_lat):
-        part = part + mom_y[d - 1]
-    mom_x_send[...] = part
-    for d in range(1, tiles_lon):
-        along_x(d, mom_x_send, mom_x.at[d - 1], mxs, mxr).start()
     for d in range(1, tiles_lon):
         along_x(d, mom_x_send, mom_x.at[d - 1], mxs, mxr).wait_recv()
     for d in range(1, tiles_lon):
@@ -352,8 +355,8 @@
             g = lam + flux_e + flux_w + flux_n + flux_s
             grad_out[s, k] = g
             edge_ew[s] = jnp.where(pair == k, column_roll(g, 2 * k + 1), edge_ew[s])
-            edge_s[pl.ds(idx, 1), :] = g[0:1]
-            edge_n[pl.ds(idx, 1), :] = g[cy - 1 : cy]
+            edge_s[pl.ds(2 * k + 1 - s, 1), :] = g[0:1]
+            edge_n[pl.ds(2 * k + 1 - s, 1), :] = g[cy - 1 : cy]
         return carry
 
     unrolled(levels, final_level, 0)
@@ -374,44 +377,77 @@
         return jnp.where(
             lane_row < LANES - off, pltpu.roll(near, back, 1), pltpu.roll(far, back, 1))
 
-    control_ids = lax.broadcasted_iota(jnp.int32, (controls, LANES), 0)
+    diagonal = lax.broadcasted_iota(jnp.int32, (cy, LANES), 0) == lax.broadcasted_iota(
+        jnp.int32, (cy, LANES), 1)
     sides = (
-        (col * cx, cx, row == 0, edge_s, None),
-        (lon + col * cx, cx, row == tiles_lat - 1, edge_n, None),
-        (2 * lon + row * cy, cy, col == 0, edge_ew, 1),
-        (2 * lon + lat + row * cy, cy, col == tiles_lon - 1, edge_ew, 0),
+        (col * cx, row == 0),
+        (lon + col * cx, row == tiles_lat - 1),
+        (2 * lon + row * cy, col == 0),
+        (2 * lon + lat + row * cy, col == tiles_lon - 1),
     )
-    ctl_send[...] = jnp.zeros(ctl_send.shape, F32)
-    for begin, count, active, edge, odd in sides:
+    for i, (begin, active) in enumerate(sides):
 
         @pl.when(active)
         def _():
-            ids = points(cmap, begin)
-            wts = jnp.where(lane_row < count, points(cwt, begin), 0.0)
-            spread = jnp.where(control_ids == ids, wts, 0.0)
-            if odd is None:
-                values, dims = edge[...], (((1,), (1,)), ((), ()))
+            wts = points(cwt, begin)
+            if i < 2:
+                values = ((edge_s, edge_n)[i][...] * wts).T
             else:
-                source = lax.broadcasted_iota(jnp.int32, (LANES, LANES), 0)
-                target = lax.broadcasted_iota(jnp.int32, (LANES, LANES), 1)
-                values, dims = jnp.zeros((cy, LANES), F32), (((1,), (0,)), ((), ()))
-                for s in range(2):
-                    level = target - s * levels
-                    move = (source == 2 * level + odd) & (level >= 0) & (level < levels)
-                    values += lax.dot_general(
-                        edge[s], move.astype(F32), dims, precision=HIGHEST,
-                        preferred_element_type=F32)
-                spread = spread[:, :cy]
-            ctl_send[...] += lax.dot_general(
-                spread, values, dims, precision=HIGHEST, preferred_element_type=F32)
+                if i == 2:
+                    values = jnp.where(even, column_roll(edge_ew[1], LANES - 1), edge_ew[0])
+                else:
+                    values = jnp.where(even, edge_ew[1], column_roll(edge_ew[0], 1))
+                weight = jnp.sum(jnp.where(diagonal, wts, 0.0), axis=1, keepdims=True)
+                values = jnp.concatenate(
+                    [values * weight, jnp.zeros((LANES - cy, LANES), F32)], axis=0)
+            high = values.astype(jnp.bfloat16)
+            rest = values - high.astype(F32)
+            middle = rest.astype(jnp.bfloat16)
+            low = (rest - middle.astype(F32)).astype(jnp.bfloat16)
+            parts[i] = jnp.concatenate([high, middle, low], axis=1)
 
     share = controls // tiles_lon
-    for d in range(1, tiles_lon):
-        begin = pl.multiple_of(lax.rem(col + d, tiles_lon) * share, 8)
-        along_x(d, ctl_send.at[pl.ds(begin, share), :], ctl_x.at[d - 1], cxs, cxr).start()
-    mine = ctl_send[pl.ds(pl.multiple_of(col * share, 8), share), :]
-    for d in range(1, tiles_lon):
-        along_x(d, ctl_send.at[pl.ds(0, share), :], ctl_x.at[d - 1], cxs, cxr).wait_recv()
+    share_ids = lax.broadcasted_iota(jnp.int32, (share, LANES), 0)
+
+    def has_points(c):
+        return (row == 0) | (row == tiles_lat - 1) | (c == 0) | (c == tiles_lon - 1)
+
+    def control_block(target):
+        start = pl.multiple_of(target * share, 8)
+        block = ctl_send.at[pl.ds(start, share), :]
+        block[...] = jnp.zeros((share, LANES), F32)
+        for i, (begin, active) in enumerate(sides):
+
+            @pl.when(active)
+            def _():
+                hit = share_ids + start == points(cmap, begin)
+                sums = lax.dot_general(
+                    jnp.where(hit, 1.0, 0.0).astype(jnp.bfloat16), parts[i],
+                    (((1,), (0,)), ((), ())), preferred_element_type=F32)
+                block[...] += (
+                    sums[:, 2 * LANES :] + sums[:, LANES : 2 * LANES]) + sums[:, :LANES]
+
+        return block
+
+    for d in range(1, tiles_lon):
+        block = control_block(lax.rem(col + d, tiles_lon))
+
+        @pl.when(has_points(col))
+        def _():
+            along_x(d, block, ctl_x.at[d - 1], cxs, cxr).start()
+
+    mine = control_block(col)[...]
+    for d in range(1, tiles_lon):
+        sender = has_points(lax.rem(col + tiles_lon - d, tiles_lon))
+
+        @pl.when(sender)
+        def _():
+            along_x(d, ctl_send.at[pl.ds(0, share), :], ctl_x.at[d - 1], cxs, cxr).wait_recv()
+
+        @pl.when(jnp.logical_not(sender))
+        def _():
+            ctl_x[d - 1] = jnp.zeros((share, LANES), F32)
+
     for d in range(1, tiles_lon):
         mine = mine + ctl_x[d - 1]
     ctl_y_send[...] = jnp.zeros(ctl_y_send.shape, F32)
@@ -424,6 +460,12 @@
         along_y(d, ctl_y_send.at[0], ctl_y.at[d - 1], cys, cyr).wait_recv()
     for d in range(1, tiles_lat):
         result = result + ctl_y[d - 1]
+    source = lax.broadcasted_iota(jnp.int32, (LANES, LANES), 0)
+    target = lax.broadcasted_iota(jnp.int32, (LANES, LANES), 1)
+    order = jnp.where(target < levels, 2 * target + 1, 2 * (target - levels))
+    result = lax.dot_general(
+        result, jnp.where(source == order, 1.0, 0.0), (((1,), (0,)), ((), ())),
+        precision=HIGHEST, preferred_element_type=F32)
     for s in range(2):
         ctrl_out[:, s, :] = result[0:CTRL_DEV, s * levels : (s + 1) * levels]
 
@@ -444,14 +486,19 @@
         along_y(d, ctl_y_send.at[0], ctl_y.at[d - 1], cys, cyr).wait_send()
     for d in range(1, tiles_lon):
         along_x(d, mom_x_send, mom_x.at[d - 1], mxs, mxr).wait_send()
-        along_x(d, ctl_send.at[pl.ds(0, share), :], ctl_x.at[d - 1], cxs, cxr).wait_send()
+
+        @pl.when(has_points(col))
+        def _():
+            along_x(d, ctl_send.at[pl.ds(0, share), :], ctl_x.at[d - 1], cxs, cxr).wait_send()
 
 
 def results_kernel(grad, surf, ctrl, grad_out, surf_out, ctrl_out, sems):
-    moves = [
-        pltpu.make_async_copy(src, dst, sems.at[i])
-        for i, (src, dst) in enumerate(((grad, grad_out), (surf, surf_out), (ctrl, ctrl_out)))
-    ]
+    half = grad.shape[1] // 2
+    pairs = [(surf, surf_out), (ctrl, ctrl_out)]
+    for s in range(2):
+        for part in (slice(0, half), slice(half, grad.shape[1])):
+            pairs.append((grad.at[s, part], grad_out.at[s, part]))
+    moves = [pltpu.make_async_copy(src, dst, sems.at[i]) for i, (src, dst) in enumerate(pairs)]
     for move in moves:
         move.start()
     for move in moves:
@@ -483,6 +530,7 @@
         buf(4, cy, cx), buf(5, cy, cx), buf(2, pack, cx), buf(3, pack, cx),
         buf(8, cx), buf(tiles_lat - 1, 8, cx), buf(8, cx), buf(tiles_lon - 1, 8, cx),
         buf(LANES, cx), buf(LANES, cx), buf(2, cy, cx),
+        pltpu.VMEM((4, LANES, 3 * LANES), jnp.bfloat16),
         buf(controls, LANES), buf(tiles_lon - 1, controls // tiles_lon, LANES),
         buf(tiles_lat, SLOT, LANES), buf(tiles_lat - 1, SLOT, LANES),
         dma((8,)), dma((8,)), dma((4,)), dma((4,)),
@@ -509,9 +557,10 @@
     grad, surf, ctrl = pl.pallas_call(
         results_kernel,
         out_shape=tuple(jax.ShapeDtypeStruct(a.shape, F32) for a in (grad, surf, ctrl)),
-        in_specs=[vmem] * 3,
+        in_specs=[pl.BlockSpec(memory_space=pl.ANY)] * 3,
         out_specs=(hbm, hbm, hbm),
-        scratch_shapes=[dma((3,))],
+        scratch_shapes=[dma((6,))],
+        compiler_params=pltpu.CompilerParams(vmem_limit_bytes=1024 * 1024),
     )(grad, surf, ctrl)
     return grad, surf, ctrl.transpose(1, 2, 0)
 

time: 38.7 us -> 36.7 us (0.948)
  local copies, waits for them, and re-layouts: 2.51 us -> 0 us
  Pallas kernels: 35.4 us -> 35.9 us
    unnamed x6 -> x0, local copies, waits for them, and re-layouts: 2.51 us -> none
    pallas_call x1, Pallas kernels: 32.5 us -> 34.5 us  [per_device(): pl.pallas_call(functools.partial(step_kernel, tiles_lon, tiles_lat, level...]
    pallas_call x1, Pallas kernels: 2.92 us -> 1.36 us  [per_device(): pl.pallas_call(results_kernel, out_shape=tuple((jax.ShapeDtypeStruct(a.sh...]
where the time goes in v3:
time: 36.7 us; the launch traced here: 36.5 us
  Pallas kernels  35.9 us (98%)
  between operations  0.64 us (2%)
    pallas_call x1, Pallas kernels, per_device(): pl.pallas_call(functools.partial(step_kernel, tiles_lon, tiles_lat, level...  34.5 us
    pallas_call x1, Pallas kernels, per_device(): pl.pallas_call(results_kernel, out_shape=tuple((jax.ShapeDtypeStruct(a.sh...  1.36 us

profile of v3, /device:TPU:0, one launch (start us, length us, event | category | flops | bytes accessed | tf_op | source)
XLA Modules:
  0.0 36.5 jit_solution(5914735280367378745)
XLA Ops:
  0.6 34.5 %shard_map.148 = (f32[2,50,40,128]{3,2,1,0:T(8,128)S(1)}, f32[40,128]{1,0:T(8,128)S(1)}, f32[10,2,50]{2,1,0:T(2,128)S(1)}) custom-call(f32[2,50,40,128]{3,2,1,0:T(8,128)} %tracer_in.1, f32[40,128]{1,0:T(8,128)} %surface_in.1, f32[50,40,128]{2,1,0:T(8,128)} %flow_e_in.1, f32[50,40,128]{2,1,0:T(8,128)} %flow_n_in.1, f32[49,40,128]{2,1,0:T(8,128)} %mix_in.1, ...), custom_call_target="tpu_custom_call" | custom-call | tf_op jit(solution)/shard_map/pallas_call | solution.py:540
  35.1 1.4 %shard_map.149 = (f32[2,50,40,128]{3,2,1,0:T(8,128)}, f32[40,128]{1,0:T(8,128)}, f32[10,2,50]{2,1,0:T(2,128)}) custom-call(f32[2,50,40,128]{3,2,1,0:T(8,128)S(1)} %get-tuple-element.9.grad, f32[40,128]{1,0:T(8,128)S(1)} %get-tuple-element.10.surf, f32[10,2,50]{2,1,0:T(2,128)S(1)} %get-tuple-element.11.ctrl), custom_call_target="tpu_custom_call" | custom-call | tf_op jit(solution)/shard_map/pallas_call | solution.py:557

commit v4 on v3

--- a/solution.py
+++ b/solution.py
@@ -88,7 +88,7 @@
     red, ratio, quad, q_e, q_w, q_n, q_s, q_c,
     pk, send_n, send_s, recv_e, recv_w, recv_n, recv_s,
     mom_send, mom_y, mom_x_send, mom_x,
-    edge_s, edge_n, edge_ew, parts,
+    pr, rr, parts, hot,
     ctl_send, ctl_x, ctl_y_send, ctl_y,
     hs, hr, ls, lr, mys, myr, mxs, mxr, cxs, cxr, cys, cyr,
 ):
@@ -141,7 +141,7 @@
         def _():
             slot[...] = jnp.zeros(slot.shape, F32)
 
-    for buf in (pk, send_n, send_s, edge_s, edge_n, edge_ew):
+    for buf in (pk, send_n, send_s, pr, rr):
         buf[...] = jnp.zeros(buf.shape, F32)
 
     for move in moves[:4]:
@@ -187,6 +187,38 @@
         @pl.when(has[i])
         def _():
             q_copy(i).start()
+
+    west, south = col == 0, row == 0
+    east_side = jnp.where(west, 0, 1)
+    lon, lat = tiles_lon * cx, tiles_lat * cy
+    controls = ctl_send.shape[0]
+    lane_row = lax.broadcasted_iota(jnp.int32, (1, LANES), 1)
+    last_chunk = cmap.shape[0] - 1
+
+    def points(ref, begin):
+        chunk = begin // LANES
+        off = lax.rem(begin, LANES)
+        near = ref[pl.ds(chunk, 1), :]
+        far = ref[pl.ds(jnp.minimum(chunk + 1, last_chunk), 1), :]
+        back = lax.rem(LANES - off, LANES)
+        return jnp.where(
+            lane_row < LANES - off, pltpu.roll(near, back, 1), pltpu.roll(far, back, 1))
+
+    for move in moves[11:]:
+        move.wait()
+    begin_row = col * cx + jnp.where(south, 0, lon)
+    begin_col = 2 * lon + row * cy + jnp.where(west, 0, lat)
+    row_on = jnp.where(south | (row == tiles_lat - 1), 1.0, 0.0)
+    col_on = jnp.where(west | (col == tiles_lon - 1), 1.0, 0.0)
+    control_ids = lax.broadcasted_iota(jnp.int32, (controls, LANES), 0)
+    for i, begin in enumerate((begin_row, begin_col)):
+        hit = jnp.where(control_ids == points(cmap, begin), 1.0, 0.0)
+        hot[:, i * LANES : (i + 1) * LANES] = hit.astype(jnp.bfloat16)
+    row_wts = points(cwt, begin_row) * row_on
+    diagonal = lax.broadcasted_iota(jnp.int32, (cy, LANES), 0) == lax.broadcasted_iota(
+        jnp.int32, (cy, LANES), 1)
+    col_wts = jnp.sum(
+        jnp.where(diagonal, points(cwt, begin_col) * col_on, 0.0), axis=1, keepdims=True)
 
     def forward(k, kap, carry):
         kap_prev, ratio_prev, r0, r1, r2, r3 = carry
@@ -203,7 +235,14 @@
         red[2, k] = r2
         red[3, k] = r3
         pk[4] = jnp.where(pair == k, column_roll(flow_e[k], 2 * k + 1), pk[4])
-        send_n[2, pl.ds(k, 1), :] = flow_n[k, cy - 1 : cy, :]
+        pr[4] = jnp.where(pair == k, column_roll(flow_e[k], 2 * k + 1 + 2 * east_side), pr[4])
+        pr[5] = jnp.where(pair == k, column_roll(flow_n[k], 2 * k + 1 + east_side), pr[5])
+        send_n[2, pl.ds(2 * k + 1, 1), :] = flow_n[k, cy - 1 : cy, :]
+        face_e = jnp.where(south, flow_e[k, 0:1, :], flow_e[k, cy - 1 : cy, :])
+        face_n = jnp.where(south, flow_n[k, 0:1, :], flow_n[k, cy - 2 : cy - 1, :])
+        for s in range(2):
+            rr[2, pl.ds(2 * k + 1 - s, 1), :] = face_e
+            rr[3, pl.ds(2 * k + 1 - s, 1), :] = face_n
         return kap, new_ratio, r0, r1, r2, r3
 
     def forward_level(k, carry):
@@ -266,10 +305,12 @@
             lam = wet * c[f]
             red[f, k] = lam
             kind, s = f // 2, f % 2
-            idx = s * levels + k
+            idx = 2 * k + 1 - s
+            pr[f] = jnp.where(pair == k, column_roll(lam, 2 * k + 3 * east_side), pr[f])
             pk[f] = jnp.where(pair == k, column_roll(lam, 2 * k + 1), pk[f])
             send_s[kind, pl.ds(idx, 1), :] = lam[0:1]
             send_n[kind, pl.ds(idx, 1), :] = lam[cy - 1 : cy]
+            rr[kind, pl.ds(idx, 1), :] = jnp.where(south, lam[1:2], lam[cy - 2 : cy - 1])
         return tuple(c)
 
     early = levels // 2
@@ -335,13 +376,83 @@
     first_lane, last_lane = lane == 0, lane == cx - 1
     first_row, last_row = sub == 0, sub == cy - 1
 
-    def final_level(k, carry):
+    filler = jnp.zeros((LANES - recv_n.shape[1], LANES), F32)
+
+    def rim_lanes(rows):
+        turned = jnp.concatenate([rows, filler], axis=0).T
+        return jnp.where(west, turned[0:1], turned[cx - 1 : cx])
+
+    north_row, south_row, south_face = (
+        rim_lanes(recv_n[0]), rim_lanes(recv_s[0]), rim_lanes(recv_s[2]))
+    x_rim = jnp.where(west, x[:cy, 0:1], x[:cy, cx - 1 : cx])
+    x_in = jnp.where(west, x[:cy, 1:2], x[:cy, cx - 2 : cx - 1])
+    half_sign = jnp.where(west, 0.5, -0.5)
+    rim_cols = []
+    for s in range(2):
+        lam = pk[s] + x_rim * pk[2 + s]
+        lam = jnp.where(west, lam, column_roll(lam, 1))
+        inner = pr[s] + x_in * pr[2 + s]
+        beyond_n = column_roll(north_row, 1) if s else north_row
+        beyond_s = column_roll(south_row, 1) if s else south_row
+        lam_n = jnp.where(last_row, beyond_n, pltpu.roll(lam, cy - 1, 0))
+        flux_n = 0.5 * pr[5] * (lam_n - lam)
+        flux_s = jnp.where(
+            first_row, 0.5 * south_face * (lam - beyond_s), pltpu.roll(flux_n, 1, 0))
+        rim_cols.append(lam + half_sign * pr[4] * (inner - lam) + flux_n + flux_s)
+    by_col = jnp.where(even, column_roll(rim_cols[1], LANES - 1), rim_cols[0]) * col_wts
+    by_col = jnp.concatenate([by_col, jnp.zeros((LANES - cy, LANES), F32)], axis=0)
+
+    side_rows = [jnp.where(south, recv_e[s, 0:1, :], recv_e[s, cy - 1 : cy, :]) for s in range(2)]
+    west_face = jnp.where(south, recv_w[4, 0:1, :], recv_w[4, cy - 1 : cy, :])
+    even_row = even[0:1]
+    turned = jnp.concatenate([
+        jnp.where(even_row, side_rows[1], column_roll(side_rows[0], 1)),
+        jnp.where(even_row, column_roll(side_rows[1], LANES - 1), side_rows[0]),
+        jnp.where(even_row, west_face, column_roll(west_face, 1)),
+        jnp.zeros((LANES - 3, LANES), F32)], axis=0).T[: rr.shape[1]]
+    x_rim = jnp.where(south, x[0:1, :cx], x[cy - 1 : cy, :cx])
+    x_in = jnp.where(south, x[1:2, :cx], x[cy - 2 : cy - 1, :cx])
+    half_sign = jnp.where(south, 0.5, -0.5)
+    lam = jnp.where(south, send_s[0], send_n[0]) + x_rim * jnp.where(south, send_s[1], send_n[1])
+    inner = rr[0] + x_in * rr[1]
+    lane_tall = lax.broadcasted_iota(jnp.int32, lam.shape, 1)
+    lam_e = jnp.where(lane_tall == cx - 1, turned[:, 0:1], column_roll(lam, cx - 1))
+    flux_e = 0.5 * rr[2] * (lam_e - lam)
+    flux_w = jnp.where(
+        lane_tall == 0, 0.5 * turned[:, 2:3] * (lam - turned[:, 1:2]), column_roll(flux_e, 1))
+    by_row = (lam + half_sign * rr[3] * (inner - lam) + flux_e + flux_w) * row_wts
+    by_row = jnp.concatenate([by_row, filler], axis=0).T
+
+    for i, values in enumerate((by_row, by_col)):
+        high = values.astype(jnp.bfloat16)
+        rest = values - high.astype(F32)
+        middle = rest.astype(jnp.bfloat16)
+        low = (rest - middle.astype(F32)).astype(jnp.bfloat16)
+        parts[i * LANES : (i + 1) * LANES] = jnp.concatenate([high, middle, low], axis=1)
+    totals = lax.dot_general(
+        hot[...], parts[...], (((1,), (0,)), ((), ())), preferred_element_type=F32)
+    ctl_send[...] = (totals[:, 2 * LANES :] + totals[:, LANES : 2 * LANES]) + totals[:, :LANES]
+
+    share = controls // tiles_lon
+
+    def has_points(c):
+        return south | (row == tiles_lat - 1) | (c == 0) | (c == tiles_lon - 1)
+
+    for d in range(1, tiles_lon):
+        begin = pl.multiple_of(lax.rem(col + d, tiles_lon) * share, 8)
+
+        @pl.when(has_points(col))
+        def _():
+            along_x(d, ctl_send.at[pl.ds(begin, share), :], ctl_x.at[d - 1], cxs, cxr).start()
+
+    def final_level(first, step, carry):
+        k = first + step
         half_e = 0.5 * flow_e[k]
         half_n = 0.5 * flow_n[k]
         half_w_halo = 0.5 * column_roll(recv_w[4], lax.rem(cx - 2 * k, cx))
-        half_s_halo = 0.5 * recv_s[2, pl.ds(k, 1), :]
+        half_s_halo = 0.5 * recv_s[2, pl.ds(2 * k + 1, 1), :]
         for s in range(2):
-            idx = s * levels + k
+            idx = 2 * k + 1 - s
             lam = red[s, k] + x_own * red[2 + s, k]
             side = column_roll(recv_e[s], cx - 1 - 2 * k)
             lam_e = jnp.where(last_lane, side, column_roll(lam, cx - 1))
@@ -354,89 +465,10 @@
             flux_s = jnp.where(first_row, halo_s, pltpu.roll(flux_n, 1, 0))
             g = lam + flux_e + flux_w + flux_n + flux_s
             grad_out[s, k] = g
-            edge_ew[s] = jnp.where(pair == k, column_roll(g, 2 * k + 1), edge_ew[s])
-            edge_s[pl.ds(2 * k + 1 - s, 1), :] = g[0:1]
-            edge_n[pl.ds(2 * k + 1 - s, 1), :] = g[cy - 1 : cy]
         return carry
 
-    unrolled(levels, final_level, 0)
-    for move in moves[11:]:
-        move.wait()
-
-    lon, lat = tiles_lon * cx, tiles_lat * cy
-    controls = ctl_send.shape[0]
-    lane_row = lax.broadcasted_iota(jnp.int32, (1, LANES), 1)
-    last_chunk = cmap.shape[0] - 1
-
-    def points(ref, begin):
-        chunk = begin // LANES
-        off = lax.rem(begin, LANES)
-        near = ref[pl.ds(chunk, 1), :]
-        far = ref[pl.ds(jnp.minimum(chunk + 1, last_chunk), 1), :]
-        back = lax.rem(LANES - off, LANES)
-        return jnp.where(
-            lane_row < LANES - off, pltpu.roll(near, back, 1), pltpu.roll(far, back, 1))
-
-    diagonal = lax.broadcasted_iota(jnp.int32, (cy, LANES), 0) == lax.broadcasted_iota(
-        jnp.int32, (cy, LANES), 1)
-    sides = (
-        (col * cx, row == 0),
-        (lon + col * cx, row == tiles_lat - 1),
-        (2 * lon + row * cy, col == 0),
-        (2 * lon + lat + row * cy, col == tiles_lon - 1),
-    )
-    for i, (begin, active) in enumerate(sides):
-
-        @pl.when(active)
-        def _():
-            wts = points(cwt, begin)
-            if i < 2:
-                values = ((edge_s, edge_n)[i][...] * wts).T
-            else:
-                if i == 2:
-                    values = jnp.where(even, column_roll(edge_ew[1], LANES - 1), edge_ew[0])
-                else:
-                    values = jnp.where(even, edge_ew[1], column_roll(edge_ew[0], 1))
-                weight = jnp.sum(jnp.where(diagonal, wts, 0.0), axis=1, keepdims=True)
-                values = jnp.concatenate(
-                    [values * weight, jnp.zeros((LANES - cy, LANES), F32)], axis=0)
-            high = values.astype(jnp.bfloat16)
-            rest = values - high.astype(F32)
-            middle = rest.astype(jnp.bfloat16)
-            low = (rest - middle.astype(F32)).astype(jnp.bfloat16)
-            parts[i] = jnp.concatenate([high, middle, low], axis=1)
-
-    share = controls // tiles_lon
-    share_ids = lax.broadcasted_iota(jnp.int32, (share, LANES), 0)
-
-    def has_points(c):
-        return (row == 0) | (row == tiles_lat - 1) | (c == 0) | (c == tiles_lon - 1)
-
-    def control_block(target):
-        start = pl.multiple_of(target * share, 8)
-        block = ctl_send.at[pl.ds(start, share), :]
-        block[...] = jnp.zeros((share, LANES), F32)
-        for i, (begin, active) in enumerate(sides):
-
-            @pl.when(active)
-            def _():
-                hit = share_ids + start == points(cmap, begin)
-                sums = lax.dot_general(
-                    jnp.where(hit, 1.0, 0.0).astype(jnp.bfloat16), parts[i],
-                    (((1,), (0,)), ((), ())), preferred_element_type=F32)
-                block[...] += (
-                    sums[:, 2 * LANES :] + sums[:, LANES : 2 * LANES]) + sums[:, :LANES]
-
-        return block
-
-    for d in range(1, tiles_lon):
-        block = control_block(lax.rem(col + d, tiles_lon))
-
-        @pl.when(has_points(col))
-        def _():
-            along_x(d, block, ctl_x.at[d - 1], cxs, cxr).start()
-
-    mine = control_block(col)[...]
+    unrolled(early, functools.partial(final_level, 0), 0)
+    mine = ctl_send[pl.ds(pl.multiple_of(col * share, 8), share), :]
     for d in range(1, tiles_lon):
         sender = has_points(lax.rem(col + tiles_lon - d, tiles_lon))
 
@@ -455,6 +487,7 @@
         ctl_y_send[j, 0:CTRL_DEV] = mine[j * CTRL_DEV : (j + 1) * CTRL_DEV]
     for d in range(1, tiles_lat):
         along_y(d, ctl_y_send.at[lax.rem(row + d, tiles_lat)], ctl_y.at[d - 1], cys, cyr).start()
+    unrolled(levels - early, functools.partial(final_level, early), 0)
     result = ctl_y_send[row]
     for d in range(1, tiles_lat):
         along_y(d, ctl_y_send.at[0], ctl_y.at[d - 1], cys, cyr).wait_recv()
@@ -529,8 +562,9 @@
         buf(5, cy, cx), buf(3, pack, cx), buf(2, pack, cx),
         buf(4, cy, cx), buf(5, cy, cx), buf(2, pack, cx), buf(3, pack, cx),
         buf(8, cx), buf(tiles_lat - 1, 8, cx), buf(8, cx), buf(tiles_lon - 1, 8, cx),
-        buf(LANES, cx), buf(LANES, cx), buf(2, cy, cx),
-        pltpu.VMEM((4, LANES, 3 * LANES), jnp.bfloat16),
+        buf(6, cy, cx), buf(4, pack, cx),
+        pltpu.VMEM((2 * LANES, 3 * LANES), jnp.bfloat16),
+        pltpu.VMEM((controls, 2 * LANES), jnp.bfloat16),
         buf(controls, LANES), buf(tiles_lon - 1, controls // tiles_lon, LANES),
         buf(tiles_lat, SLOT, LANES), buf(tiles_lat - 1, SLOT, LANES),
         dma((8,)), dma((8,)), dma((4,)), dma((4,)),

time: 36.7 us -> 32.8 us (0.89)
  Pallas kernels: 35.9 us -> 32 us
    pallas_call x1, Pallas kernels: 34.5 us -> 30.6 us  [per_device(): pl.pallas_call(functools.partial(step_kernel, tiles_lon, tiles_lat, level...]
where the time goes in v4:
time: 32.8 us; the launch traced here: 32.6 us
  Pallas kernels  32 us (98%)
  between operations  0.64 us (2%)
    pallas_call x1, Pallas kernels, per_device(): pl.pallas_call(functools.partial(step_kernel, tiles_lon, tiles_lat, level...  30.6 us
    pallas_call x1, Pallas kernels, per_device(): pl.pallas_call(results_kernel, out_shape=tuple((jax.ShapeDtypeStruct(a.sh...  1.36 us

profile of v4, /device:TPU:0, one launch (start us, length us, event | category | flops | bytes accessed | tf_op | source)
XLA Modules:
  0.0 32.6 jit_solution(601764692362021789)
XLA Ops:
  0.6 30.6 %shard_map.148 = (f32[2,50,40,128]{3,2,1,0:T(8,128)S(1)}, f32[40,128]{1,0:T(8,128)S(1)}, f32[10,2,50]{2,1,0:T(2,128)S(1)}) custom-call(f32[2,50,40,128]{3,2,1,0:T(8,128)} %tracer_in.1, f32[40,128]{1,0:T(8,128)} %surface_in.1, f32[50,40,128]{2,1,0:T(8,128)} %flow_e_in.1, f32[50,40,128]{2,1,0:T(8,128)} %flow_n_in.1, f32[49,40,128]{2,1,0:T(8,128)} %mix_in.1, ...), custom_call_target="tpu_custom_call" | custom-call | tf_op jit(solution)/shard_map/pallas_call | solution.py:574
  31.3 1.4 %shard_map.149 = (f32[2,50,40,128]{3,2,1,0:T(8,128)}, f32[40,128]{1,0:T(8,128)}, f32[10,2,50]{2,1,0:T(2,128)}) custom-call(f32[2,50,40,128]{3,2,1,0:T(8,128)S(1)} %get-tuple-element.9.grad, f32[40,128]{1,0:T(8,128)S(1)} %get-tuple-element.10.surf, f32[10,2,50]{2,1,0:T(2,128)S(1)} %get-tuple-element.11.ctrl), custom_call_target="tpu_custom_call" | custom-call | tf_op jit(solution)/shard_map/pallas_call | solution.py:591

commit v5 on v4

--- a/solution.py
+++ b/solution.py
@@ -188,6 +188,40 @@
         def _():
             q_copy(i).start()
 
+    quarter = levels // 16 * 4
+    bounds = (levels, 3 * quarter, 2 * quarter, quarter, 0)
+    l_table = [
+        (0, pk.at[4], recv_w.at[4]), (2, send_n.at[2], recv_s.at[2]),
+        (0, pk.at[0:4], recv_w.at[0:4]), (1, pk.at[0:4], recv_e),
+    ]
+    for high, low in zip(bounds[:-1], bounds[1:]):
+        rows = pl.ds(2 * low, (send_s.shape[1] if high == levels else 2 * high) - 2 * low)
+        l_table.append((2, send_n.at[0:2, rows, :], recv_s.at[0:2, rows, :]))
+        l_table.append((3, send_s.at[0:2, rows, :], recv_n.at[0:2, rows, :]))
+
+    def l_copy(e):
+        i, src, dst = l_table[e]
+        dx, dy = DIRS[i]
+        return pltpu.make_async_remote_copy(
+            src_ref=src, dst_ref=dst, send_sem=ls.at[e], recv_sem=lr.at[e],
+            device_id=(col + dx, row + dy), device_id_type=MESH)
+
+    def l_start(e):
+        @pl.when(has[l_table[e][0]])
+        def _():
+            l_copy(e).start()
+
+    def l_arrive(e):
+        o = OPPOSITE[l_table[e][0]]
+        dst = l_table[e][2]
+        dx, dy = DIRS[o]
+
+        @pl.when(has[o])
+        def _():
+            pltpu.make_async_remote_copy(
+                src_ref=dst, dst_ref=dst, send_sem=ls.at[e], recv_sem=lr.at[e],
+                device_id=(col + dx, row + dy), device_id_type=MESH).wait_recv()
+
     west, south = col == 0, row == 0
     east_side = jnp.where(west, 0, 1)
     lon, lat = tiles_lon * cx, tiles_lat * cy
@@ -254,6 +288,8 @@
     zero = jnp.zeros((cy, cx), F32)
     carry = unrolled(levels - 1, forward_level, (zero,) * 6)
     forward(levels - 1, zero, carry)
+    l_start(0)
+    l_start(1)
 
     for i in range(8):
 
@@ -313,38 +349,23 @@
             rr[kind, pl.ds(idx, 1), :] = jnp.where(south, lam[1:2], lam[cy - 2 : cy - 1])
         return tuple(c)
 
-    early = levels // 2
-    lower = unrolled(early, functools.partial(backward_level, 0), (zero,) * 4)
-    part = mom_send[...]
-    for d in range(1, tiles_lat):
-        along_y(d, mom_send, mom_y.at[d - 1], mys, myr).wait_recv()
-    for d in range(1, tiles_lat):
-        part = part + mom_y[d - 1]
-    mom_x_send[...] = part
-    for d in range(1, tiles_lon):
-        along_x(d, mom_x_send, mom_x.at[d - 1], mxs, mxr).start()
-    unrolled(levels - early, functools.partial(backward_level, early), lower)
-
-    l_src = [pk, pk.at[0:4], send_n, send_s]
-
-    def l_copy(i):
-        dx, dy = DIRS[i]
-        o = OPPOSITE[i]
-        return pltpu.make_async_remote_copy(
-            src_ref=l_src[i], dst_ref=l_slots[o], send_sem=ls.at[i], recv_sem=lr.at[o],
-            device_id=(col + dx, row + dy), device_id_type=MESH)
-
-    def l_arrival(i):
-        dx, dy = DIRS[i]
-        return pltpu.make_async_remote_copy(
-            src_ref=l_slots[i], dst_ref=l_slots[i], send_sem=ls.at[i], recv_sem=lr.at[i],
-            device_id=(col + dx, row + dy), device_id_type=MESH)
-
-    for i in range(4):
-
-        @pl.when(has[i])
-        def _():
-            l_copy(i).start()
+    columns = (zero,) * 4
+    for part_no, (high, low) in enumerate(zip(bounds[:-1], bounds[1:])):
+        columns = unrolled(
+            high - low, functools.partial(backward_level, levels - high), columns)
+        l_start(4 + 2 * part_no)
+        l_start(5 + 2 * part_no)
+        if part_no == 1:
+            part = mom_send[...]
+            for d in range(1, tiles_lat):
+                along_y(d, mom_send, mom_y.at[d - 1], mys, myr).wait_recv()
+            for d in range(1, tiles_lat):
+                part = part + mom_y[d - 1]
+            mom_x_send[...] = part
+            for d in range(1, tiles_lon):
+                along_x(d, mom_x_send, mom_x.at[d - 1], mxs, mxr).start()
+    l_start(2)
+    l_start(3)
 
     for d in range(1, tiles_lon):
         along_x(d, mom_x_send, mom_x.at[d - 1], mxs, mxr).wait_recv()
@@ -356,11 +377,8 @@
     x_own = x[:cy, :cx]
     surf_out[...] = x_own
 
-    for i in range(4):
-
-        @pl.when(has[i])
-        def _():
-            l_arrival(i).wait_recv()
+    for e in range(len(l_table)):
+        l_arrive(e)
 
     even = lane == 2 * pair
     x_e, x_w = x[:cy, cx : cx + 1], x[:cy, 2 * cx - 1 : 2 * cx]
@@ -467,6 +485,7 @@
             grad_out[s, k] = g
         return carry
 
+    early = levels // 2
     unrolled(early, functools.partial(final_level, 0), 0)
     mine = ctl_send[pl.ds(pl.multiple_of(col * share, 8), share), :]
     for d in range(1, tiles_lon):
@@ -508,11 +527,11 @@
         def _():
             q_copy(i).wait_send()
 
-    for i in range(4):
-
-        @pl.when(has[i])
-        def _():
-            l_copy(i).wait_send()
+    for e in range(len(l_table)):
+
+        @pl.when(has[l_table[e][0]])
+        def _():
+            l_copy(e).wait_send()
 
     for d in range(1, tiles_lat):
         along_y(d, mom_send, mom_y.at[d - 1], mys, myr).wait_send()
@@ -567,7 +586,7 @@
         pltpu.VMEM((controls, 2 * LANES), jnp.bfloat16),
         buf(controls, LANES), buf(tiles_lon - 1, controls // tiles_lon, LANES),
         buf(tiles_lat, SLOT, LANES), buf(tiles_lat - 1, SLOT, LANES),
-        dma((8,)), dma((8,)), dma((4,)), dma((4,)),
+        dma((8,)), dma((8,)), dma((12,)), dma((12,)),
         dma((tiles_lat - 1,)), dma((tiles_lat - 1,)), dma((tiles_lon - 1,)), dma((tiles_lon - 1,)),
         dma((tiles_lon - 1,)), dma((tiles_lon - 1,)), dma((tiles_lat - 1,)), dma((tiles_lat - 1,)),
     ]

time: 32.8 us -> 29.9 us (0.912)
  Pallas kernels: 32 us -> 29.1 us
    pallas_call x1, Pallas kernels: 30.6 us -> 27.8 us  [per_device(): pl.pallas_call(functools.partial(step_kernel, tiles_lon, tiles_lat, level...]
where the time goes in v5:
time: 29.9 us; the launch traced here: 29.8 us
  Pallas kernels  29.1 us (97%)
  between operations  0.64 us (2%)
    pallas_call x1, Pallas kernels, per_device(): pl.pallas_call(functools.partial(step_kernel, tiles_lon, tiles_lat, level...  27.8 us
    pallas_call x1, Pallas kernels, per_device(): pl.pallas_call(results_kernel, out_shape=tuple((jax.ShapeDtypeStruct(a.sh...  1.36 us

profile of v5, /device:TPU:0, one launch (start us, length us, event | category | flops | bytes accessed | tf_op | source)
XLA Modules:
  0.0 29.8 jit_solution(3198668861043575808)
XLA Ops:
  0.6 27.8 %shard_map.148 = (f32[2,50,40,128]{3,2,1,0:T(8,128)S(1)}, f32[40,128]{1,0:T(8,128)S(1)}, f32[10,2,50]{2,1,0:T(2,128)S(1)}) custom-call(f32[2,50,40,128]{3,2,1,0:T(8,128)} %tracer_in.1, f32[40,128]{1,0:T(8,128)} %surface_in.1, f32[50,40,128]{2,1,0:T(8,128)} %flow_e_in.1, f32[50,40,128]{2,1,0:T(8,128)} %flow_n_in.1, f32[49,40,128]{2,1,0:T(8,128)} %mix_in.1, ...), custom_call_target="tpu_custom_call" | custom-call | tf_op jit(solution)/shard_map/pallas_call | solution.py:593
  28.4 1.4 %shard_map.149 = (f32[2,50,40,128]{3,2,1,0:T(8,128)}, f32[40,128]{1,0:T(8,128)}, f32[10,2,50]{2,1,0:T(2,128)}) custom-call(f32[2,50,40,128]{3,2,1,0:T(8,128)S(1)} %get-tuple-element.9.grad, f32[40,128]{1,0:T(8,128)S(1)} %get-tuple-element.10.surf, f32[10,2,50]{2,1,0:T(2,128)S(1)} %get-tuple-element.11.ctrl), custom_call_target="tpu_custom_call" | custom-call | tf_op jit(solution)/shard_map/pallas_call | solution.py:610

commit v6 on v5

--- a/solution.py
+++ b/solution.py
@@ -18,8 +18,12 @@
 HIGHEST = lax.Precision.HIGHEST
 
 
+def step_width(count):
+    return max(u for u in range(1, 8) if count % u == 0)
+
+
 def unrolled(count, body, carry):
-    width = max(u for u in range(1, 8) if count % u == 0)
+    width = step_width(count)
 
     def several(i, carry):
         for u in range(width):
@@ -331,28 +335,32 @@
     for d in range(1, tiles_lat):
         along_y(d, mom_send, mom_y.at[d - 1], mys, myr).start()
 
-    def backward_level(first, step, carry):
-        k = levels - 1 - first - step
+    def backward_group(width, first, i, carry):
         c = list(carry)
-        wet = mask[k].astype(F32)
-        rat = ratio[k]
         for f in range(4):
-            c[f] = red[f, k] + rat * c[f]
-            lam = wet * c[f]
-            red[f, k] = lam
             kind, s = f // 2, f % 2
-            idx = 2 * k + 1 - s
-            pr[f] = jnp.where(pair == k, column_roll(lam, 2 * k + 3 * east_side), pr[f])
-            pk[f] = jnp.where(pair == k, column_roll(lam, 2 * k + 1), pk[f])
-            send_s[kind, pl.ds(idx, 1), :] = lam[0:1]
-            send_n[kind, pl.ds(idx, 1), :] = lam[cy - 1 : cy]
-            rr[kind, pl.ds(idx, 1), :] = jnp.where(south, lam[1:2], lam[cy - 2 : cy - 1])
+            outer, inner = pk[f], pr[f]
+            for u in range(width):
+                k = levels - 1 - first - (i * width + u)
+                idx = 2 * k + 1 - s
+                c[f] = red[f, k] + ratio[k] * c[f]
+                lam = mask[k].astype(F32) * c[f]
+                red[f, k] = lam
+                inner = jnp.where(pair == k, column_roll(lam, 2 * k + 3 * east_side), inner)
+                outer = jnp.where(pair == k, column_roll(lam, 2 * k + 1), outer)
+                send_s[kind, pl.ds(idx, 1), :] = lam[0:1]
+                send_n[kind, pl.ds(idx, 1), :] = lam[cy - 1 : cy]
+                rr[kind, pl.ds(idx, 1), :] = jnp.where(south, lam[1:2], lam[cy - 2 : cy - 1])
+            pk[f] = outer
+            pr[f] = inner
         return tuple(c)
 
     columns = (zero,) * 4
     for part_no, (high, low) in enumerate(zip(bounds[:-1], bounds[1:])):
-        columns = unrolled(
-            high - low, functools.partial(backward_level, levels - high), columns)
+        width = step_width(high - low)
+        columns = lax.fori_loop(
+            0, (high - low) // width,
+            functools.partial(backward_group, width, levels - high), columns)
         l_start(4 + 2 * part_no)
         l_start(5 + 2 * part_no)
         if part_no == 1:

time: 29.9 us -> 30 us (level)
  no operation moved by 1% of the time
where the time goes in v6:
time: 30 us; the launch traced here: 29.9 us
  Pallas kernels  29.2 us (97%)
  between operations  0.64 us (2%)
    pallas_call x1, Pallas kernels, per_device(): pl.pallas_call(functools.partial(step_kernel, tiles_lon, tiles_lat, level...  27.9 us
    pallas_call x1, Pallas kernels, per_device(): pl.pallas_call(results_kernel, out_shape=tuple((jax.ShapeDtypeStruct(a.sh...  1.36 us

profile of v6, /device:TPU:0, one launch (start us, length us, event | category | flops | bytes accessed | tf_op | source)
XLA Modules:
  0.0 29.9 jit_solution(13511697376963112048)
XLA Ops:
  0.6 27.9 %shard_map.148 = (f32[2,50,40,128]{3,2,1,0:T(8,128)S(1)}, f32[40,128]{1,0:T(8,128)S(1)}, f32[10,2,50]{2,1,0:T(2,128)S(1)}) custom-call(f32[2,50,40,128]{3,2,1,0:T(8,128)} %tracer_in.1, f32[40,128]{1,0:T(8,128)} %surface_in.1, f32[50,40,128]{2,1,0:T(8,128)} %flow_e_in.1, f32[50,40,128]{2,1,0:T(8,128)} %flow_n_in.1, f32[49,40,128]{2,1,0:T(8,128)} %mix_in.1, ...), custom_call_target="tpu_custom_call" | custom-call | tf_op jit(solution)/shard_map/pallas_call | solution.py:601
  28.5 1.4 %shard_map.149 = (f32[2,50,40,128]{3,2,1,0:T(8,128)}, f32[40,128]{1,0:T(8,128)}, f32[10,2,50]{2,1,0:T(2,128)}) custom-call(f32[2,50,40,128]{3,2,1,0:T(8,128)S(1)} %get-tuple-element.9.grad, f32[40,128]{1,0:T(8,128)S(1)} %get-tuple-element.10.surf, f32[10,2,50]{2,1,0:T(2,128)S(1)} %get-tuple-element.11.ctrl), custom_call_target="tpu_custom_call" | custom-call | tf_op jit(solution)/shard_map/pallas_call | solution.py:618
